TPU v7x, 128 devices: a whole 4x4x4 slice. The times are simulated.
128 devices in a mesh: front: 8 (over z, x_lo), row: 8 (over x_hi, y), col: 2 (over core).
Axes of the slice: x: 4 (x_hi: 2, x_lo: 2; x = x_hi * 2 + x_lo), y: 4, z: 4, core: 2. Of those that a mesh axis runs over, the one named last changes fastest.
Arguments:
- front_matrix: float32 [8, 12, 1024, 3072], P('front', None, 'row', 'col')
- front_sizes: int32 [8], P('front'), may hold values from 8192 to 12288, as said below
- contrib: float32 [8, 4, 1024, 3072], P('front', None, 'row', 'col'), may hold values from -6 to 6
- dest_front: int32 [8, 4, 8], P('front', None, 'row'), may hold values from 0 to 7, as said below
- dest_local: int32 [8, 4, 8], P('front', None, 'row'), may hold values from 1 to 11, as said below
Outputs:
- factored: float32 [8, 12, 1024, 3072], P('front', None, 'row', 'col')
Inputs may be any that keep to these rules, and one draw needn't show every extreme that they name: `front_sizes`: multiples of 128; every draw has a front of order 12288 and one of order 8192. For each (g, r), the 4 entries dest_front[g, :, r] name distinct fronts. The block (g, k, r) lands on parent rows from (dest_local * 8 + r) * 128: at or after row 1024 and wholly below the parent's order; several blocks may land on the same rows; in every draw some block lands in the last round of blocks of the largest front.
All inputs are finite; a program needn't handle non-finite values.
Results may differ from a plain program's by a relative error of at most 0.0003.
Values sent between devices are 32-bit elements; how exact they have to be, the bound alone decides.
A program may use at most 128 MiB of HBM per device.

v0:
```python
import jax
import jax.numpy as jnp
from jax import lax
from jax.sharding import PartitionSpec as P

PW = 512
NPANEL = 2
W = 3072


def broadcast(value, axis, source):
    kept = jnp.where(lax.axis_index(axis) == source, value, 0).astype(value.dtype)
    return lax.psum(kept, axis)


def lower_inverse(pivot_block):
    symmetric = jnp.tril(pivot_block) + jnp.tril(pivot_block, -1).T
    factor = jnp.linalg.cholesky(symmetric)
    eye_block = jnp.eye(factor.shape[0], dtype=jnp.float32)
    inverse = jax.scipy.linalg.solve_triangular(factor, eye_block, lower=True)
    return (factor, inverse)


def on_device(front_matrix, front_sizes, contrib, dest_front, dest_local):
    front_count = lax.axis_size("front")
    row_count = lax.axis_size("row")
    row_here = lax.axis_index("row")
    col_here = lax.axis_index("col")
    local_blocks = front_matrix.shape[1]
    block_rows = front_matrix.shape[2]
    half_width = front_matrix.shape[3]
    half_rows = block_rows // 2
    cycle_rows = row_count * block_rows
    local_rows = local_blocks * block_rows
    window_blocks = W // cycle_rows
    block_ids = jnp.arange(local_blocks, dtype=jnp.int32)
    global_row = (
        block_ids[:, None] * cycle_rows
        + row_here * block_rows
        + jnp.arange(block_rows, dtype=jnp.int32)[None, :]
    ).reshape(local_rows)
    global_col = col_here * half_width + jnp.arange(half_width, dtype=jnp.int32)
    matrix = front_matrix[0].reshape(local_rows, half_width)
    matrix = jnp.where((global_row < front_sizes[0])[:, None], matrix, 0.0)
    targets = dest_front[0, :, 0]
    places = dest_local[0, :, 0]
    fronts_all = jnp.arange(front_count, dtype=jnp.int32)
    select = targets[None, :] == fronts_all[:, None]
    outgoing = jnp.einsum(
        "fk,kiw->fiw", select.astype(jnp.float32), contrib[0], precision=lax.Precision.HIGHEST
    )
    slot_place = jnp.where(
        jnp.any(select, axis=1), jnp.sum(jnp.where(select, places[None, :], 0), axis=1), -1
    )
    incoming, in_place = (
        lax.all_to_all(outgoing, "front", split_axis=0, concat_axis=0, tiled=True),
        lax.all_to_all(slot_place, "front", split_axis=0, concat_axis=0, tiled=True),
    )
    placing = (in_place[None, :] == block_ids[:, None]).astype(jnp.float32)
    placed_rows = jnp.einsum("ls,siw->liw", placing, incoming, precision=lax.Precision.HIGHEST)
    matrix = matrix + placed_rows.reshape(local_rows, half_width)
    for panel_index in range(NPANEL):
        col_start = panel_index * PW
        owned_columns = matrix[:, col_start : col_start + PW]
        columns = broadcast(owned_columns, "col", 0)
        first_block = col_start // block_rows
        pivot_block = first_block // row_count
        offset = first_block % row_count * block_rows
        col_blocks = columns.reshape(local_blocks, block_rows, PW)
        row_piece = lax.dynamic_slice_in_dim(
            col_blocks[pivot_block], col_here * half_rows, half_rows, 0
        )
        gathered = lax.all_gather(row_piece, ("row", "col"), axis=0, tiled=True)
        factor, inverse = lower_inverse(gathered[offset : offset + PW])
        solved = jnp.dot(columns, inverse.T, precision=lax.Precision.HIGHEST)
        solved = jnp.where((global_row < col_start)[:, None], 0.0, solved)
        global_first = (pivot_block * row_count + row_here) * block_rows
        in_pivot = (global_first >= col_start) & (global_first < col_start + PW)
        pivot_piece = lax.dynamic_slice_in_dim(
            factor, jnp.clip(global_first - col_start, 0, PW - block_rows), block_rows, 0
        )
        current = solved[pivot_block * block_rows : (pivot_block + 1) * block_rows]
        solved = solved.at[pivot_block * block_rows : (pivot_block + 1) * block_rows].set(
            jnp.where(in_pivot, pivot_piece, current)
        )
        solved_blocks = solved.reshape(local_blocks, block_rows, PW)
        row_piece = lax.dynamic_slice_in_dim(
            solved_blocks[:window_blocks], col_here * half_rows, half_rows, 1
        )
        window_factor = lax.all_gather(row_piece, ("row", "col"), axis=1, tiled=True).reshape(W, PW)
        mine_cols = lax.dynamic_slice_in_dim(window_factor, col_here * half_width, half_width, 0)
        update = jnp.dot(solved, mine_cols.T, precision=lax.Precision.HIGHEST)
        active = (global_row >= col_start + PW)[:, None] & (global_col >= col_start + PW)[None, :]
        matrix = matrix - jnp.where(active, update, 0.0)
        replaced = jnp.where(col_here == 0, solved, matrix[:, col_start : col_start + PW])
        matrix = matrix.at[:, col_start : col_start + PW].set(replaced)
    upper_part = (global_row < NPANEL * PW)[:, None] & (global_col >= NPANEL * PW)[None, :]
    matrix = jnp.where(upper_part, 0.0, matrix)
    return matrix.reshape(1, local_blocks, block_rows, half_width)


def solution(mesh):
    return jax.shard_map(
        on_device,
        mesh=mesh,
        in_specs=(
            P("front", None, "row", "col"),
            P("front"),
            P("front", None, "row", "col"),
            P("front", None, "row"),
            P("front", None, "row"),
        ),
        out_specs=P("front", None, "row", "col"),
        check_vma=False,
    )
```

profile of v0, /device:TPU:1, one launch (start us, length us, event | category | flops | bytes accessed | tf_op | source)
XLA Modules:
  0.0 793.3 jit_solution(2299873840947495213)
XLA Ops:
  8.9 6.8 all-to-all-start
  15.7 6.5 fusion.4
  22.2 6.3 copy.24
  28.6 5.1 all-to-all-start.1
  35.2 69.0 %all-to-all-done.1 = f32[8,128,1536]{2,1,0:T(8,128)} async-done(((f32[8,128,1536]{2,1,0:T(8,128)}), f32[8,128,1536]{2,1,0:T(8,128)}, u32[]{:S(2)}, u32[]{:S(2)}) %all-to-all-start.1) | async-done | bytes 6291488 | tf_op jit(solution)/shard_map/all_to_all | solution.py:56
  104.2 12.9 %fusion = f32[12,128,1536]{2,0,1:T(8,128)} fusion(f32[8,128,1536]{2,1,0:T(8,128)} %all-to-all-done.1, s32[8]{0:T(128)S(1)} %reduce.34), kind=kOutput, calls=%fused_computation.9 | convolution fusion | flops 226492512 | bytes 15728672 | tf_op jit(solution)/shard_map/ls,siw->liw/dot_general | solution.py:60
  117.1 13.8 %copy.26 = f32[12,128,1536]{2,1,0:T(8,128)} copy(f32[12,128,1536]{2,0,1:T(8,128)} %fusion) | data formatting | bytes 18874368 | tf_op jit(solution)/shard_map/ls,siw->liw/dot_general | solution.py:60
  130.9 11.0 %bitcast_add_fusion = f32[1536,1536]{1,0:T(8,128)} fusion(f32[12,128,1536]{2,1,0:T(8,128)} %copy.26, f32[1,12,128,1536]{3,2,1,0:T(8,128)} %param.16, pred[1536]{0:T(1024)(128)(4,1)S(1)} %get-tuple-element.120), kind=kLoop, calls=%fused_computation.4 | loop fusion | flops 4718592 | bytes 28313088 | tf_op jit(solution)/shard_map/add | solution.py:61
  141.9 3.9 slice_select_fusion.1
  145.9 30.6 %all-reduce.4.cloned.1.call-done = f32[1536,512]{1,0:T(8,128)} async-done(((f32[1536,512]{1,0:T(8,128)}), f32[1536,512]{1,0:T(8,128)}) %all-reduce.4.cloned.1.call-update) | async-done | bytes 3145744 | tf_op jit(solution)/shard_map/psum | solution.py:13
  178.5 49.5 %all-gather.5.cloned.1.call-done = f32[1024,512]{1,0:T(8,128)} async-done(((f32[64,512]{1,0:T(8,128)}), f32[1024,512]{1,0:T(8,128)}) %all-gather.5.cloned.1.call-update) | async-done | bytes 2097168 | tf_op jit(solution)/shard_map/all_gather | solution.py:73
  229.7 1.4 bitcast_add_fusion.4
  232.7 11.7 %cholesky.286 = f32[128,128]{1,0:T(8,128)S(1)} custom-call(f32[128,128]{1,0:T(8,128)S(1)} %cholesky.426), custom_call_target="Cholesky" | custom-call | tf_op jit(solution)/shard_map/jit(cholesky)/cholesky | solution.py:18
  244.4 9.8 %custom-call.27 = f32[1,128,128]{1,2,0:T(8,128)S(1)} custom-call(f32[1,128,128]{2,1,0:T(8,128)S(1)} %get-tuple-element.114), custom_call_target="InvertDiagBlocksLowerTriangular" | custom-call | tf_op jit(solution)/shard_map/jit(cholesky)/cholesky | solution.py:18
  256.9 11.7 %cholesky.305 = f32[128,128]{1,0:T(8,128)S(1)} custom-call(f32[128,128]{1,0:T(8,128)S(1)} %cholesky.430), custom_call_target="Cholesky" | custom-call | tf_op jit(solution)/shard_map/jit(cholesky)/cholesky | solution.py:18
  268.6 10.0 %custom-call.28 = f32[1,128,128]{1,2,0:T(8,128)S(1)} custom-call(f32[1,128,128]{2,1,0:T(8,128)S(1)} %get-tuple-element.111), custom_call_target="InvertDiagBlocksLowerTriangular" | custom-call | tf_op jit(solution)/shard_map/jit(cholesky)/cholesky | solution.py:18
  280.2 11.7 %cholesky.326 = f32[128,128]{1,0:T(8,128)S(1)} custom-call(f32[128,128]{1,0:T(8,128)S(1)} %cholesky.435), custom_call_target="Cholesky" | custom-call | tf_op jit(solution)/shard_map/jit(cholesky)/cholesky | solution.py:18
  292.7 9.8 %custom-call.29 = f32[1,128,128]{1,2,0:T(8,128)S(1)} custom-call(f32[1,128,128]{2,1,0:T(8,128)S(1)} %get-tuple-element.108), custom_call_target="InvertDiagBlocksLowerTriangular" | custom-call | tf_op jit(solution)/shard_map/jit(cholesky)/cholesky | solution.py:18
  303.9 12.1 %cholesky.343 = f32[128,128]{1,0:T(8,128)S(1)} custom-call(f32[128,128]{1,0:T(8,128)S(1)} %convolution_subtract_fusion.11), custom_call_target="Cholesky" | custom-call | tf_op jit(solution)/shard_map/jit(cholesky)/cholesky | solution.py:18
  321.3 8.4 %while.8 = (s32[]{:T(128)}, f32[512,512]{1,0:T(8,128)S(1)}, s32[4,2]{0,1:T(2,128)S(1)}, f32[4,128,128]{2,1,0:T(8,128)S(1)}, s32[]{:T(128)}) while((s32[]{:T(128)}, f32[512,512]{1,0:T(8,128)S(1)}, s32[4,2]{0,1:T(2,128)S(1)}, f32[4,128,128]{2,1,0:T(8,128)S(1)}, s32[]{:T(128)}) %tuple.74), condition=%wide.while_cond.4, body=%wide.while_body.4.sunk | while | flops 2 | bytes 131181 | solution.py:20
  322.0 1.4 bitcast_dynamic-update-slice_fusion.4
  324.1 1.4 bitcast_dynamic-update-slice_fusion.4
  326.2 1.4 bitcast_dynamic-update-slice_fusion.4
  328.3 1.4 bitcast_dynamic-update-slice_fusion.4
  329.8 39.3 %custom-call.30 = f32[4,128,128]{1,2,0:T(8,128)S(1)} custom-call(f32[4,128,128]{2,1,0:T(8,128)S(1)} %get-tuple-element.69), custom_call_target="InvertDiagBlocksLowerTriangular" | custom-call | tf_op jit(solution)/shard_map/jit(_solve_triangular)/triangular_solve | solution.py:20
  372.2 7.1 convolution_select_fusion.1
  382.1 62.1 %all-gather.7.cloned.1.call-done = f32[3,1024,512]{2,1,0:T(8,128)} async-done(((f32[3,64,512]{2,1,0:T(8,128)}), f32[3,1024,512]{2,1,0:T(8,128)}) %all-gather.7.cloned.1.call-update) | async-done | bytes 6291472 | tf_op jit(solution)/shard_map/all_gather | solution.py:90
  444.2 19.2 %select_subtract_fusion.1 = f32[1536,1536]{1,0:T(8,128)S(1)} fusion(f32[1536,1536]{1,0:T(8,128)} %bitcast_add_fusion, f32[1536,512]{1,0:T(8,128)S(1)} %fusion.46, pred[1536]{0:T(1024)(128)(4,1)S(1)} %fusion.84, pred[1536]{0:T(1024)(128)(4,1)S(1)} %get-tuple-element.119, f32[3072,512]{1,0:T(8,128)} %bitcast.143, s32[]{:T(128)S(6)} %select_n.117), kind=kOutput, calls=%fused_computation.7 | convolution fusion | flops 14502592512 | bytes 25168900 | tf_op jit(solution)/shard_map/dot_general | solution.py:92
  463.4 1.5 fusion.2
  464.9 3.7 copy-done.2
  468.7 2.1 slice_select_fusion
  470.8 26.8 %all-reduce.6.cloned.1.call-done = f32[1536,512]{1,0:T(8,128)} async-done(((f32[1536,512]{1,0:T(8,128)}), f32[1536,512]{1,0:T(8,128)}) %all-reduce.6.cloned.1.call-update) | async-done | bytes 3145744 | tf_op jit(solution)/shard_map/psum | solution.py:13
  500.0 48.7 %all-gather.9.cloned.1.call-done = f32[1024,512]{1,0:T(8,128)} async-done(((f32[64,512]{1,0:T(8,128)}), f32[1024,512]{1,0:T(8,128)}) %all-gather.9.cloned.1.call-update) | async-done | bytes 2097168 | tf_op jit(solution)/shard_map/all_gather | solution.py:73
  550.4 1.4 bitcast_add_fusion.2
  552.4 11.7 %cholesky.358 = f32[128,128]{1,0:T(8,128)S(1)} custom-call(f32[128,128]{1,0:T(8,128)S(1)} %cholesky.439), custom_call_target="Cholesky" | custom-call | tf_op jit(solution)/shard_map/jit(cholesky)/cholesky | solution.py:18
  564.3 9.8 %custom-call.31 = f32[1,128,128]{1,2,0:T(8,128)S(1)} custom-call(f32[1,128,128]{2,1,0:T(8,128)S(1)} %get-tuple-element.104), custom_call_target="InvertDiagBlocksLowerTriangular" | custom-call | tf_op jit(solution)/shard_map/jit(cholesky)/cholesky | solution.py:18
  574.8 11.7 %cholesky.377 = f32[128,128]{1,0:T(8,128)S(1)} custom-call(f32[128,128]{1,0:T(8,128)S(1)} %cholesky.443), custom_call_target="Cholesky" | custom-call | tf_op jit(solution)/shard_map/jit(cholesky)/cholesky | solution.py:18
  587.8 10.2 %custom-call.32 = f32[1,128,128]{1,2,0:T(8,128)S(1)} custom-call(f32[1,128,128]{2,1,0:T(8,128)S(1)} %get-tuple-element.101), custom_call_target="InvertDiagBlocksLowerTriangular" | custom-call | tf_op jit(solution)/shard_map/jit(cholesky)/cholesky | solution.py:18
  598.7 11.7 %cholesky.398 = f32[128,128]{1,0:T(8,128)S(1)} custom-call(f32[128,128]{1,0:T(8,128)S(1)} %cholesky.448), custom_call_target="Cholesky" | custom-call | tf_op jit(solution)/shard_map/jit(cholesky)/cholesky | solution.py:18
  611.1 9.8 %custom-call.33 = f32[1,128,128]{1,2,0:T(8,128)S(1)} custom-call(f32[1,128,128]{2,1,0:T(8,128)S(1)} %get-tuple-element.98), custom_call_target="InvertDiagBlocksLowerTriangular" | custom-call | tf_op jit(solution)/shard_map/jit(cholesky)/cholesky | solution.py:18
  621.5 11.8 %cholesky.415 = f32[128,128]{1,0:T(8,128)S(1)} custom-call(f32[128,128]{1,0:T(8,128)S(1)} %convolution_subtract_fusion.10), custom_call_target="Cholesky" | custom-call | tf_op jit(solution)/shard_map/jit(cholesky)/cholesky | solution.py:18
  637.9 8.1 %while.9 = (s32[]{:T(128)}, f32[512,512]{1,0:T(8,128)S(1)}, s32[4,2]{0,1:T(2,128)S(1)}, f32[4,128,128]{2,1,0:T(8,128)S(1)}, s32[]{:T(128)}) while((s32[]{:T(128)}, f32[512,512]{1,0:T(8,128)S(1)}, s32[4,2]{0,1:T(2,128)S(1)}, f32[4,128,128]{2,1,0:T(8,128)S(1)}, s32[]{:T(128)}) %tuple.92), condition=%wide.while_cond.4.clone, body=%wide.while_body.4.clone.sunk | while | flops 2 | bytes 131181 | solution.py:20
  646.0 39.3 %custom-call.34 = f32[4,128,128]{1,2,0:T(8,128)S(1)} custom-call(f32[4,128,128]{2,1,0:T(8,128)S(1)} %get-tuple-element.70), custom_call_target="InvertDiagBlocksLowerTriangular" | custom-call | tf_op jit(solution)/shard_map/jit(_solve_triangular)/triangular_solve | solution.py:20
  688.5 7.1 convolution_select_fusion
  698.2 62.2 %all-gather.11.cloned.1.call-done = f32[3,1024,512]{2,1,0:T(8,128)} async-done(((f32[3,64,512]{2,1,0:T(8,128)}), f32[3,1024,512]{2,1,0:T(8,128)}) %all-gather.11.cloned.1.call-update) | async-done | bytes 6291472 | tf_op jit(solution)/shard_map/all_gather | solution.py:90
  760.5 19.3 %select_subtract_fusion = f32[1536,1536]{1,0:T(8,128)S(1)} fusion(f32[1536,1536]{1,0:T(8,128)} %copy-done.2, f32[1536,512]{1,0:T(8,128)S(1)} %fusion.44, pred[1536]{0:T(1024)(128)(4,1)S(1)} %fusion.85, pred[1536]{0:T(1024)(128)(4,1)S(1)} %get-tuple-element.117, f32[3072,512]{1,0:T(8,128)} %bitcast.144, s32[]{:T(128)S(6)} %select_n.117), kind=kOutput, calls=%fused_computation.6 | convolution fusion | flops 14502592512 | bytes 25168900 | tf_op jit(solution)/shard_map/dot_general | solution.py:92
  779.8 1.6 fusion.3
  781.4 4.7 and_select_fusion
  (132 shorter events, 50.7 us)
Async XLA Ops:
  6.5 9.2 %copy-start = (f32[1,4,128,1536]{3,2,1,0:T(8,128)S(1)}, f32[1,4,128,1536]{3,2,1,0:T(8,128)}, u32[]{:S(2)}) copy-start(f32[1,4,128,1536]{3,2,1,0:T(8,128)} %param.18) | copy-start | bytes 9437188
  8.9 19.6 %all-to-all-start = ((s32[8,1,1]{2,1,0:T(1,128)}), s32[8,1,1]{2,1,0:T(1,128)S(1)}, u32[]{:S(2)}, u32[]{:S(2)}) async-start(s32[8,1,1]{2,1,0:T(1,128)} %copy.22), calls=%async_computation | async-start | bytes 8192 | tf_op jit(solution)/shard_map/all_to_all | solution.py:57
  28.6 75.7 %all-to-all-start.1 = ((f32[8,128,1536]{2,1,0:T(8,128)}), f32[8,128,1536]{2,1,0:T(8,128)}, u32[]{:S(2)}, u32[]{:S(2)}) async-start(f32[8,128,1536]{2,1,0:T(8,128)} %copy.24), calls=%async_computation.1 | async-start | bytes 12582912 | tf_op jit(solution)/shard_map/all_to_all | solution.py:56
  33.7 142.8 %all-reduce.4.cloned.1.call-start = ((), (), s32[]{:S(2)}) async-start(), calls=%async_computation.2 | async-start | bytes 6291456 | tf_op jit(solution)/shard_map/psum | solution.py:13
  145.8 82.2 %all-gather.5.cloned.1.call-start = ((), (), s32[]{:S(2)}) async-start(), calls=%async_computation.3 | async-start | bytes 2228224 | tf_op jit(solution)/shard_map/all_gather | solution.py:73
  178.1 266.1 %all-gather.7.cloned.1.call-start = ((), (), s32[]{:S(2)}) async-start(), calls=%async_computation.4 | async-start | bytes 6684672 | tf_op jit(solution)/shard_map/all_gather | solution.py:90
  178.5 192.7 %copy-start.3 = (f32[512,512]{1,0:T(8,128)}, f32[512,512]{1,0:T(8,128)S(1)}, u32[]{:S(2)}) copy-start(f32[512,512]{1,0:T(8,128)S(1)} %fusion.27) | copy-start | bytes 3145732
  231.7 1.0 copy-start.5
  381.2 116.3 %all-reduce.6.cloned.1.call-start = ((), (), s32[]{:S(2)}) async-start(), calls=%async_computation.5 | async-start | bytes 6291456 | tf_op jit(solution)/shard_map/psum | solution.py:13
  464.9 3.7 copy-start.2
  470.8 77.9 %all-gather.9.cloned.1.call-start = ((), (), s32[]{:S(2)}) async-start(), calls=%async_computation.6 | async-start | bytes 2228224 | tf_op jit(solution)/shard_map/all_gather | solution.py:73
  499.2 261.2 %all-gather.11.cloned.1.call-start = ((), (), s32[]{:S(2)}) async-start(), calls=%async_computation.7 | async-start | bytes 6684672 | tf_op jit(solution)/shard_map/all_gather | solution.py:90
  586.5 98.8 %copy-start.4 = (f32[512,512]{1,0:T(8,128)S(1)}, f32[512,512]{1,0:T(8,128)}, u32[]{:S(2)}) copy-start(f32[512,512]{1,0:T(8,128)} %copy-done.3) | copy-start | bytes 3145732
  781.4 4.8 copy-start.1
Sparse Core Ops, SparseCore 0:
  145.9 30.4 all-reduce.3
  179.2 48.7 all-gather.4
  381.4 62.7 all-gather.6
  470.9 26.6 all-reduce.5
  499.9 48.7 all-gather.8
  697.6 62.7 all-gather.10
where the time goes:
time: 802 us; the launch traced here: 793 us
  waiting for transfers between devices  349 us (44%)
  other arithmetic  275 us (34%)
  matrix products  85.6 us (11%)
  local copies, waits for them, and re-layouts  50.2 us (6%)
  between operations  20.2 us (3%)
  starting transfers between devices  13.2 us (2%)
    another operation x29, other arithmetic, lower_inverse(): factor = jnp.linalg.cholesky(symmetric)  159 us
    all_gather x2, waiting for transfers between devices, on_device(): lax.all_gather(row_piece, ('row', 'col'), axis=1, tiled=True).reshape(W, PW)  124 us
    all_gather x2, waiting for transfers between devices, on_device(): gathered = lax.all_gather(row_piece, ('row', 'col'), axis=0, tiled=True)  98.2 us
    another operation x5, other arithmetic, lower_inverse(): inverse = jax.scipy.linalg.solve_triangular(factor, eye_block, lower=True)  81.1 us
    all_to_all x1, waiting for transfers between devices, on_device(): lax.all_to_all(outgoing, 'front', split_axis=0, concat_axis=0, tiled=True)  69 us
    psum x2, waiting for transfers between devices, broadcast(): return lax.psum(kept, axis)  57.3 us
    dot_general x2, matrix products, on_device(): update = jnp.dot(solved, mine_cols.T, precision=lax.Precision.HIGHEST)  38.5 us
    another operation x27, local copies, waits for them, and re-layouts, lower_inverse(): inverse = jax.scipy.linalg.solve_triangular(factor, eye_block, lower=True)  16.4 us
  transfers between devices with their start and end apart: 8, of which 7 were waited for; matrix products, arithmetic and copies ran while one was open for 2% of the time, Pallas kernels for 0%

commit v1 on v0

v1 whole, which is shorter than its diff:
```python
import functools

import jax
import jax.numpy as jnp
from jax import lax
from jax.experimental import pallas as pl
from jax.experimental.pallas import tpu as pltpu
from jax.sharding import PartitionSpec as P

F = 8
R = 8
B = 128
LB = 12
HW = 1536
PC = 1024
NB = PC // B
KD = 256
MESH = pl.DeviceIdType.MESH
ANY = pl.BlockSpec(memory_space=pl.ANY)
VM = pl.BlockSpec(memory_space=pltpu.VMEM)
F32 = jnp.float32
MIB = 2**20


def split(x):
    hi = x.astype(jnp.bfloat16)
    return hi, (x - hi.astype(F32)).astype(jnp.bfloat16)


def left3(hi, lo):
    return jnp.concatenate([hi, lo, hi], 1)


def right3(hi, lo):
    return jnp.concatenate([hi, hi, lo], 1)


def dot_nt(a, b):
    return lax.dot_general(a, b, (((1,), (1,)), ((), ())), preferred_element_type=F32)


def dot_nn(a, b):
    return lax.dot_general(a, b, (((1,), (0,)), ((), ())), preferred_element_type=F32)


def dot3(a, b):
    return dot_nt(left3(*split(a)), right3(*split(b)))


def dot3_nn(a, b):
    bh, bl = split(b)
    return dot_nn(left3(*split(a)), jnp.concatenate([bh, bh, bl], 0))


def pack_kernel(which_ref, in_ref, out_ref):
    out_ref[...] = in_ref[...]


def pack(contrib, which):
    return pl.pallas_call(
        pack_kernel,
        grid_spec=pltpu.PrefetchScalarGridSpec(
            num_scalar_prefetch=1,
            grid=(F,),
            in_specs=[pl.BlockSpec((1, B, HW), lambda f, which: (which[f], 0, 0))],
            out_specs=pl.BlockSpec((1, B, HW), lambda f, which: (f, 0, 0)),
        ),
        out_shape=jax.ShapeDtypeStruct((F, B, HW), F32),
    )(which, contrib)


def first_exchange(front_ref, pack_ref, place_ref, piv_ref, inc_ref, got_ref, psend, precv, fsend, asend, arecv, lsend, lrecv, local):
    f = lax.axis_index("front")
    r = lax.axis_index("row")
    c = lax.axis_index("col")
    barrier = pltpu.get_barrier_semaphore()

    for d in range(1, F):
        pl.semaphore_signal(barrier, inc=1, device_id={"front": lax.rem(f + d, F)}, device_id_type=MESH)
    pl.semaphore_signal(barrier, inc=1, device_id={"col": 1 - c}, device_id_type=MESH)

    @pl.when(c == 0)
    def _():
        for d in range(1, R):
            pl.semaphore_signal(barrier, inc=1, device_id={"row": lax.rem(r + d, R)}, device_id_type=MESH)
        pl.semaphore_wait(barrier, F - 1 + 1 + R - 1)

    @pl.when(c == 1)
    def _():
        pl.semaphore_wait(barrier, F - 1 + 1)

    def pivot_copy(i, d):
        w = (i + 1) * B
        return pltpu.make_async_remote_copy(
            src_ref=front_ref.at[0, :, pl.ds(0, w)],
            dst_ref=piv_ref.at[i, :, pl.ds(0, w)],
            send_sem=psend.at[d],
            recv_sem=precv.at[i],
            device_id={"row": lax.rem(r + d, R)},
            device_id_type=MESH,
        )

    def pivot_own(i):
        w = (i + 1) * B
        return pltpu.make_async_copy(front_ref.at[0, :, pl.ds(0, w)], piv_ref.at[i, :, pl.ds(0, w)], local.at[0])

    def pivot_hand(i, own):
        w = (i + 1) * B
        return pltpu.make_async_remote_copy(
            src_ref=front_ref.at[0, :, pl.ds(0, w)] if own else piv_ref.at[i, :, pl.ds(0, w)],
            dst_ref=piv_ref.at[i, :, pl.ds(0, w)],
            send_sem=fsend.at[i],
            recv_sem=precv.at[i],
            device_id={"col": 1},
            device_id_type=MESH,
        )

    def contrib_copy(d):
        to = lax.rem(f + d, F)
        return pltpu.make_async_remote_copy(
            src_ref=pack_ref.at[to, :, pl.ds(0, PC)],
            dst_ref=inc_ref.at[f, :, pl.ds(0, PC)],
            send_sem=asend.at[d],
            recv_sem=arecv.at[d],
            device_id={"front": to},
            device_id_type=MESH,
        )

    def place_copy(d):
        to = lax.rem(f + d, F)
        return pltpu.make_async_remote_copy(
            src_ref=place_ref.at[to],
            dst_ref=got_ref.at[f],
            send_sem=lsend.at[d],
            recv_sem=lrecv.at[d],
            device_id={"front": to},
            device_id_type=MESH,
        )

    @pl.when(c == 0)
    def _():
        for i in range(R):
            @pl.when(r == i)
            def _():
                for d in range(1, R):
                    pivot_copy(i, d).start()
                pivot_hand(i, True).start()
                pivot_own(i).start()
        for d in range(1, F):
            contrib_copy(d).start()

    for d in range(1, F):
        place_copy(d).start()
    own_inc = pltpu.make_async_copy(pack_ref.at[f], inc_ref.at[f], local.at[1])
    own_inc.start()
    own_place = pltpu.make_async_copy(place_ref.at[f], got_ref.at[f], local.at[2])
    own_place.start()

    @pl.when(c == 0)
    def _():
        for i in range(R):
            @pl.when(r != i)
            def _():
                pivot_hand(i, False).wait_recv()
                pivot_hand(i, False).start()
        for i in range(R):
            @pl.when(r == i)
            def _():
                for d in range(1, R):
                    pivot_copy(i, d).wait_send()
                pivot_own(i).wait()
            pivot_hand(i, False).wait_send()
        for d in range(1, F):
            contrib_copy(d).wait()

    @pl.when(c == 1)
    def _():
        for i in range(R):
            pivot_hand(i, False).wait_recv()

    for d in range(1, F):
        place_copy(d).wait()
    own_inc.wait()
    own_place.wait()


def exchange_one(front, packed, places):
    return pl.pallas_call(
        first_exchange,
        out_shape=(
            jax.ShapeDtypeStruct((R, B, PC), F32),
            jax.ShapeDtypeStruct((F, B, HW), F32),
            jax.ShapeDtypeStruct((F, 8, 128), jnp.int32),
        ),
        in_specs=[ANY] * 3,
        out_specs=(ANY,) * 3,
        scratch_shapes=[
            pltpu.SemaphoreType.DMA((R,)),
            pltpu.SemaphoreType.DMA((R,)),
            pltpu.SemaphoreType.DMA((R,)),
            pltpu.SemaphoreType.DMA((F,)),
            pltpu.SemaphoreType.DMA((F,)),
            pltpu.SemaphoreType.DMA((F,)),
            pltpu.SemaphoreType.DMA((F,)),
            pltpu.SemaphoreType.DMA((3,)),
        ],
        compiler_params=pltpu.CompilerParams(collective_id=0, has_side_effects=True),
    )(front, packed, places)


def second_exchange(panel_ref, pack_ref, own_ref, win_ref, inc_ref, ssend, srecv, wsend, wrecv, vsend, vrecv, asend, arecv, local):
    f = lax.axis_index("front")
    r = lax.axis_index("row")
    c = lax.axis_index("col")
    barrier = pltpu.get_barrier_semaphore()

    for d in range(1, F):
        pl.semaphore_signal(barrier, inc=1, device_id={"front": lax.rem(f + d, F)}, device_id_type=MESH)
    for d in range(R):
        pl.semaphore_signal(barrier, inc=1, device_id={"row": lax.rem(r + d, R), "col": 1 - c}, device_id_type=MESH)

    @pl.when(c == 0)
    def _():
        for d in range(1, R):
            pl.semaphore_signal(barrier, inc=1, device_id={"row": lax.rem(r + d, R)}, device_id_type=MESH)
        pl.semaphore_wait(barrier, F - 1 + R + R - 1)

    @pl.when(c == 1)
    def _():
        pl.semaphore_wait(barrier, F - 1 + R)

    hand = pltpu.make_async_remote_copy(
        src_ref=panel_ref, dst_ref=own_ref, send_sem=ssend, recv_sem=srecv, device_id={"col": 1}, device_id_type=MESH
    )

    def second_round(d):
        return pltpu.make_async_remote_copy(
            src_ref=panel_ref.at[1],
            dst_ref=win_ref.at[4 + r],
            send_sem=wsend.at[d],
            recv_sem=wrecv.at[d],
            device_id={"row": lax.rem(r + d, R), "col": 1},
            device_id_type=MESH,
        )

    def first_round_high(d):
        return pltpu.make_async_remote_copy(
            src_ref=panel_ref.at[0],
            dst_ref=win_ref.at[r - 4],
            send_sem=vsend.at[d],
            recv_sem=vrecv.at[r - 4],
            device_id={"row": lax.rem(r + d, R), "col": 1},
            device_id_type=MESH,
        )

    def first_round_low(d):
        return pltpu.make_async_remote_copy(
            src_ref=panel_ref.at[0],
            dst_ref=win_ref.at[r],
            send_sem=vsend.at[d],
            recv_sem=vrecv.at[r],
            device_id={"row": lax.rem(r + d, R)},
            device_id_type=MESH,
        )

    def landed(i):
        return pltpu.make_async_remote_copy(
            src_ref=panel_ref.at[0],
            dst_ref=win_ref.at[i],
            send_sem=vsend.at[0],
            recv_sem=vrecv.at[i],
            device_id={"col": 1 - c},
            device_id_type=MESH,
        )

    def contrib_low(d):
        to = lax.rem(f + d, F)
        return pltpu.make_async_remote_copy(
            src_ref=pack_ref.at[to, :, pl.ds(PC, HW - PC)],
            dst_ref=inc_ref.at[f, :, pl.ds(PC, HW - PC)],
            send_sem=asend.at[d],
            recv_sem=arecv.at[d],
            device_id={"front": to},
            device_id_type=MESH,
        )

    def contrib_high(d):
        to = lax.rem(f + d, F)
        return pltpu.make_async_remote_copy(
            src_ref=pack_ref.at[to],
            dst_ref=inc_ref.at[f],
            send_sem=asend.at[d],
            recv_sem=arecv.at[d],
            device_id={"front": to},
            device_id_type=MESH,
        )

    keep_win = pltpu.make_async_copy(panel_ref.at[0], win_ref.at[lax.rem(r, 4)], local.at[0])
    keep_own = pltpu.make_async_copy(panel_ref, own_ref, local.at[1])
    own_inc = pltpu.make_async_copy(pack_ref.at[f], inc_ref.at[f], local.at[2])

    @pl.when(c == 0)
    def _():
        for d in range(R):
            second_round(d).start()

        @pl.when(r >= 4)
        def _():
            for d in range(R):
                first_round_high(d).start()

        @pl.when(r < 4)
        def _():
            for d in range(1, R):
                first_round_low(d).start()
            keep_win.start()

        hand.start()
        for d in range(1, F):
            contrib_low(d).start()
        keep_own.start()

    @pl.when(c == 1)
    def _():
        for d in range(1, F):
            contrib_high(d).start()

    own_inc.start()

    @pl.when(c == 0)
    def _():
        for d in range(R):
            second_round(d).wait_send()

        @pl.when(r >= 4)
        def _():
            for d in range(R):
                first_round_high(d).wait_send()

        @pl.when(r < 4)
        def _():
            for d in range(1, R):
                first_round_low(d).wait_send()
            keep_win.wait()

        for i in range(4):
            @pl.when(r != i)
            def _():
                landed(i).wait_recv()

        hand.wait_send()
        for d in range(1, F):
            contrib_low(d).wait()
        keep_own.wait()

    @pl.when(c == 1)
    def _():
        hand.wait_recv()
        for d in range(R):
            second_round(d).wait_recv()
        for i in range(4):
            landed(i).wait_recv()
        for d in range(1, F):
            contrib_high(d).wait()

    own_inc.wait()


def exchange_two(panel, packed):
    return pl.pallas_call(
        second_exchange,
        out_shape=(
            jax.ShapeDtypeStruct((LB - 1, B, PC), F32),
            jax.ShapeDtypeStruct((12, B, PC), F32),
            jax.ShapeDtypeStruct((F, B, HW), F32),
        ),
        in_specs=[ANY] * 2,
        out_specs=(ANY,) * 3,
        scratch_shapes=[
            pltpu.SemaphoreType.DMA,
            pltpu.SemaphoreType.DMA,
            pltpu.SemaphoreType.DMA((R,)),
            pltpu.SemaphoreType.DMA((R,)),
            pltpu.SemaphoreType.DMA((R,)),
            pltpu.SemaphoreType.DMA((4,)),
            pltpu.SemaphoreType.DMA((F,)),
            pltpu.SemaphoreType.DMA((F,)),
            pltpu.SemaphoreType.DMA((3,)),
        ],
        compiler_params=pltpu.CompilerParams(collective_id=1, has_side_effects=True),
    )(panel, packed)


def assemble_kernel(meta_ref, front_ref, inc_ref, out_ref):
    lb = pl.program_id(0) + 1
    valid = (lb * R + meta_ref[0]) * B < meta_ref[2]
    out_ref[...] = jnp.where(valid, front_ref[...], 0.0)
    for s in range(F):
        @pl.when(meta_ref[3 + s] == lb)
        def _():
            out_ref[...] += inc_ref[s : s + 1]


def assemble(meta, front, inc):
    return pl.pallas_call(
        assemble_kernel,
        grid_spec=pltpu.PrefetchScalarGridSpec(
            num_scalar_prefetch=1,
            grid=(LB - 1,),
            in_specs=[
                pl.BlockSpec((1, B, PC), lambda i, meta: (i + 1, 0, 0)),
                pl.BlockSpec((F, B, PC), lambda i, meta: (0, 0, 0)),
            ],
            out_specs=pl.BlockSpec((1, B, PC), lambda i, meta: (i, 0, 0)),
        ),
        out_shape=jax.ShapeDtypeStruct((LB - 1, B, PC), F32),
        compiler_params=pltpu.CompilerParams(vmem_limit_bytes=32 * MIB),
    )(meta, front, inc)


def recip(x):
    first = pl.reciprocal(x, approx=True)
    return first * (2.0 - x * first)


def lane_spread(x, k):
    return jnp.broadcast_to(x[:, k : k + 1], (8, B))


def row_spread(x, j):
    return jnp.broadcast_to(x[j : j + 1, :], (8, B))


def factor_block(sym):
    sub = lax.broadcasted_iota(jnp.int32, (8, B), 0)
    lane = lax.broadcasted_iota(jnp.int32, (8, B), 1)
    count = B // 8
    rows = [sym[q * 8 : (q + 1) * 8, :] for q in range(count)]
    eyes = [jnp.where(lane == sub + q * 8, 1.0, 0.0).astype(F32) for q in range(count)]
    factor, inverse = [], []
    for p in range(count):
        v, e = rows[p], eyes[p]
        c = [lane_spread(v, p * 8 + k) for k in range(8)]
        more = p < count - 1
        if more:
            v2, e2 = rows[p + 1], eyes[p + 1]
            c2 = [lane_spread(v2, p * 8 + k) for k in range(8)]
        diagonal = None
        for j in range(8):
            pivot = row_spread(c[j], j)
            diagonal = pivot if diagonal is None else jnp.where(sub == j, pivot, diagonal)
            over = recip(pivot)
            rv, re = row_spread(v, j), row_spread(e, j)
            m = jnp.where(sub > j, c[j] * over, 0.0)
            if more:
                m2 = c2[j] * over
            for k in range(j + 1, 8):
                s = row_spread(c[k], j)
                c[k] = c[k] - m * s
                if more:
                    c2[k] = c2[k] - m2 * s
            v = v - m * rv
            e = e - m * re
            if more:
                v2 = v2 - m2 * rv
                e2 = e2 - m2 * re
        scale = lax.rsqrt(diagonal)
        factor.append(jnp.where(lane >= sub + p * 8, v * scale, 0.0))
        inverse.append(e * scale)
        if more:
            rows[p + 1], eyes[p + 1] = v2, e2
        if p < count - 2:
            t = (v * recip(diagonal)).T
            rv = [row_spread(v, j) for j in range(8)]
            re = [row_spread(e, j) for j in range(8)]
            for q in range(p + 2, count):
                tq = t[q * 8 : (q + 1) * 8, :]
                for j in range(8):
                    m = jnp.broadcast_to(tq[:, j : j + 1], (8, B))
                    rows[q] = rows[q] - m * rv[j]
                    eyes[q] = eyes[q] - m * re[j]
    return jnp.concatenate(factor, 0), jnp.concatenate(inverse, 0)


def cholesky_kernel(a_ref, l_ref, i_ref, x_ref):
    l_ref[...] = a_ref[...]
    row_id = lax.broadcasted_iota(jnp.int32, (B, B), 0)
    col_id = lax.broadcasted_iota(jnp.int32, (B, B), 1)

    def step(k, carry):
        o = pl.multiple_of(k * B, B)
        d = l_ref[pl.ds(o, B), pl.ds(o, B)]
        lt, li = factor_block(jnp.where(row_id >= col_id, d, d.T))
        l_ref[pl.ds(o, B), pl.ds(o, B)] = lt.T
        x_ref[k] = li

        def trailing(kk):
            def run():
                base = (kk + 1) * B
                x = dot3(l_ref[base:, kk * B : base], li)
                l_ref[base:, kk * B : base] = x
                xh, xl = split(x)
                xa, xb = left3(xh, xl), right3(xh, xl)
                for j in range(kk + 1, NB):
                    jo = (j - kk - 1) * B
                    l_ref[j * B :, j * B : (j + 1) * B] -= dot_nt(xa[jo:], xb[jo : jo + B])

            return run

        for kk in range(NB - 1):
            pl.when(k == kk)(trailing(kk))
        return carry

    lax.fori_loop(0, NB, step, 0)
    for i in range(NB - 1):
        l_ref[i * B : (i + 1) * B, (i + 1) * B :] = jnp.zeros((B, (NB - 1 - i) * B), F32)
    for i in range(NB // 2):
        low, high = x_ref[2 * i], x_ref[2 * i + 1]
        between = l_ref[(2 * i + 1) * B : (2 * i + 2) * B, 2 * i * B : (2 * i + 1) * B]
        i_ref[i, :B, :B] = low
        i_ref[i, :B, B:] = jnp.zeros((B, B), F32)
        i_ref[i, B:, :B] = -dot3_nn(high, dot3_nn(between, low))
        i_ref[i, B:, B:] = high


def cholesky(a):
    return pl.pallas_call(
        cholesky_kernel,
        out_shape=(
            jax.ShapeDtypeStruct((PC, PC), F32),
            jax.ShapeDtypeStruct((PC // KD, KD, KD), F32),
        ),
        in_specs=[VM],
        out_specs=(VM, VM),
        scratch_shapes=[pltpu.VMEM((NB, B, B), F32)],
        compiler_params=pltpu.CompilerParams(vmem_limit_bytes=48 * MIB),
    )(a)


def final_kernel(meta_ref, front_ref, inc_ref, panel_ref, win_ref, l_ref, i_ref, out_ref, ph, plo, wh, wl, l3):
    t = pl.program_id(0)
    col = meta_ref[1]
    steps = PC // KD

    def solve(blocks, source_ref, hi_ref, lo_ref, at):
        rows = blocks * B
        his, los = [], []
        for k in range(steps):
            cols = slice(k * KD, (k + 1) * KD)
            a = source_ref[pl.ds(at, blocks), :, cols].reshape(rows, KD)
            for m in range(k):
                a = a - dot_nt(
                    left3(his[m], los[m]), l3[cols, 3 * m * KD : 3 * (m + 1) * KD]
                )
            p = dot3(a, i_ref[k])
            hi, lo = split(p)
            his.append(hi)
            los.append(lo)
            hi_ref[pl.ds(at * B, rows), cols] = hi
            lo_ref[pl.ds(at * B, rows), cols] = lo

    @pl.when(t == 0)
    def _():
        for m in range(steps - 1):
            hi, lo = split(l_ref[:, m * KD : (m + 1) * KD])
            l3[:, 3 * m * KD : 3 * (m + 1) * KD] = right3(hi, lo)
        solve(6, panel_ref, ph, plo, 0)
        solve(5, panel_ref, ph, plo, 6)
        solve(4, win_ref, wh, wl, 0)

        @pl.when(col == 1)
        def _():
            solve(4, win_ref, wh, wl, 4)
            solve(4, win_ref, wh, wl, 8)

    @pl.when((col == 0) & (t < steps))
    def _():
        row = pl.multiple_of(meta_ref[0] * B, B)
        for k in range(steps):
            @pl.when(t == k)
            def _():
                cols = slice(k * KD, (k + 1) * KD)
                out_ref[0] = l_ref[pl.ds(row, B), cols]
                out_ref[1:] = (ph[:, cols].astype(F32) + plo[:, cols].astype(F32)).reshape(LB - 1, B, KD)

    @pl.when((col == 1) | (t >= steps))
    def _():
        start = pl.multiple_of((t - jnp.where(col == 0, steps, 0)) * KD, KD)
        w_hi, w_lo = wh[pl.ds(start, KD), :], wl[pl.ds(start, KD), :]
        update = dot_nt(ph[...], w_hi) + dot_nt(plo[...], w_hi) + dot_nt(ph[...], w_lo)
        out_ref[0] = jnp.zeros((B, KD), F32)
        for lb in range(1, LB):
            valid = (lb * R + meta_ref[0]) * B < meta_ref[2]
            out_ref[lb] = jnp.where(valid, front_ref[lb], 0.0) - update[(lb - 1) * B : lb * B]
        for s in range(F):
            place = meta_ref[3 + s]

            @pl.when(place >= 0)
            def _():
                out_ref[pl.ds(place, 1)] += inc_ref[s : s + 1]


def final(meta, front, inc, panel, win, low, inv):
    tiles = HW // KD
    whole = dict(pipeline_mode=pl.Buffered(1))
    return pl.pallas_call(
        final_kernel,
        grid_spec=pltpu.PrefetchScalarGridSpec(
            num_scalar_prefetch=1,
            grid=(tiles,),
            in_specs=[
                pl.BlockSpec((LB, B, KD), lambda t, meta: (0, 0, t)),
                pl.BlockSpec((F, B, KD), lambda t, meta: (0, 0, t)),
                pl.BlockSpec((LB - 1, B, PC), lambda t, meta: (0, 0, 0), **whole),
                pl.BlockSpec((12, B, PC), lambda t, meta: (0, 0, 0), **whole),
                pl.BlockSpec((PC, PC), lambda t, meta: (0, 0), **whole),
                pl.BlockSpec((PC // KD, KD, KD), lambda t, meta: (0, 0, 0), **whole),
            ],
            out_specs=pl.BlockSpec((LB, B, KD), lambda t, meta: (0, 0, t)),
            scratch_shapes=[
                pltpu.VMEM(((LB - 1) * B, PC), jnp.bfloat16),
                pltpu.VMEM(((LB - 1) * B, PC), jnp.bfloat16),
                pltpu.VMEM((12 * B, PC), jnp.bfloat16),
                pltpu.VMEM((12 * B, PC), jnp.bfloat16),
                pltpu.VMEM((PC, 3 * (PC - KD)), jnp.bfloat16),
            ],
        ),
        out_shape=jax.ShapeDtypeStruct((LB, B, HW), F32),
        compiler_params=pltpu.CompilerParams(vmem_limit_bytes=60 * MIB),
    )(meta, front, inc, panel, win, low, inv)


def on_device(front_matrix, front_sizes, contrib, dest_front, dest_local):
    front = front_matrix[0]
    targets = dest_front[0, :, 0]
    places = dest_local[0, :, 0]
    select = targets[None, :] == jnp.arange(F, dtype=jnp.int32)[:, None]
    which = jnp.sum(jnp.where(select, jnp.arange(4, dtype=jnp.int32)[None, :], 0), axis=1)
    slot_place = jnp.where(jnp.any(select, axis=1), jnp.sum(jnp.where(select, places[None, :], 0), axis=1), -1)
    packed = pack(contrib[0], which)
    sent_places = jnp.broadcast_to(slot_place[:, None, None], (F, 8, 128))
    pivot, inc, got = exchange_one(front, packed, sent_places)
    row_col = jnp.stack([lax.axis_index("row"), lax.axis_index("col"), front_sizes[0]]).astype(jnp.int32)
    meta = jnp.concatenate([row_col, got[:, 0, 0]])
    panel = assemble(meta, front, inc)
    own, win, inc_rest = exchange_two(panel, packed)
    low, inv = cholesky(pivot.reshape(PC, PC))
    out = final(meta, front, inc_rest, own, win, low, inv)
    return out[None]


def solution(mesh):
    return jax.shard_map(
        on_device,
        mesh=mesh,
        in_specs=(
            P("front", None, "row", "col"),
            P("front"),
            P("front", None, "row", "col"),
            P("front", None, "row"),
            P("front", None, "row"),
        ),
        out_specs=P("front", None, "row", "col"),
        check_vma=False,
    )
```

time: 802 us -> 389 us (0.49)
  the two profiles are of different devices: /device:TPU:1 before, /device:TPU:0 now
where the time goes in v1:
time: 389 us; the launch traced here: 388 us
  Pallas kernels  372 us (96%)
  local copies, waits for them, and re-layouts  13.6 us (3%)
    pallas_call x1, Pallas kernels, exchange_two(): pl.pallas_call(second_exchange, out_shape=(jax.ShapeDtypeStruct((LB - 1,...  243 us
    pallas_call x1, Pallas kernels, cholesky(): pl.pallas_call(cholesky_kernel, out_shape=(jax.ShapeDtypeStruct((PC, PC),...  49.4 us
    pallas_call x1, Pallas kernels, exchange_one(): pl.pallas_call(first_exchange, out_shape=(jax.ShapeDtypeStruct((R, B, PC)...  39 us
    pallas_call x1, Pallas kernels, final(): pl.pallas_call(final_kernel, grid_spec=pltpu.PrefetchScalarGridSpec(num_s...  29.7 us
    unnamed x14, local copies, waits for them, and re-layouts  12 us
    pallas_call x1, Pallas kernels, pack(): pl.pallas_call(pack_kernel, grid_spec=pltpu.PrefetchScalarGridSpec(num_sc...  8.73 us

profile of v1, /device:TPU:0, one launch (start us, length us, event | category | flops | bytes accessed | tf_op | source)
XLA Modules:
  0.0 388.2 jit_solution(4403410756165242392)
XLA Ops:
  0.0 0.0 copy-start.6
  0.0 1.4 select_reduce_fusion
  1.4 8.7 %shard_map.55.pack_ref = f32[8,128,1536]{2,1,0:T(8,128)} custom-call(s32[8]{0:T(128)} %get-tuple-element.22.which_ref, f32[4,128,1536]{2,1,0:T(8,128)} %bitcast.12), custom_call_target="tpu_custom_call" | custom-call | tf_op jit(solution)/shard_map/pallas_call | solution.py:60
  10.1 0.0 copy-done.6
  10.1 0.1 fusion
  10.2 0.7 broadcast_in_dim.40.place_ref
  10.9 39.0 %shard_map.56 = (f32[8,128,1024]{2,1,0:T(8,128)}, f32[8,128,1536]{2,1,0:T(8,128)}, s32[8,8,128]{2,1,0:T(8,128)}) custom-call(f32[12,128,1536]{2,1,0:T(8,128)} %bitcast.8, f32[8,128,1536]{2,1,0:T(8,128)} %shard_map.55.pack_ref, s32[8,8,128]{2,1,0:T(8,128)} %broadcast_in_dim.40.place_ref), custom_call_target="tpu_custom_call" | custom-call | tf_op jit(solution)/shard_map/pallas_call | solution.py:188
  49.9 1.0 slice_reduce_fusion
  51.5 0.1 pad_add_fusion.meta_ref
  51.6 0.0 copy-start.5
  51.6 0.0 copy-start
  51.6 3.7 copy-done
  55.3 0.0 copy-start.2
  55.3 2.8 copy-done.2
  58.1 3.0 shard_map.57.panel_ref
  61.0 0.0 copy-done.5
  61.1 0.0 copy-start.1
  61.1 2.5 copy-done.1
  63.6 242.6 %shard_map.58 = (f32[11,128,1024]{2,1,0:T(8,128)}, f32[12,128,1024]{2,1,0:T(8,128)}, f32[8,128,1536]{2,1,0:T(8,128)}) custom-call(f32[11,128,1024]{2,1,0:T(8,128)} %copy-done.1, f32[8,128,1536]{2,1,0:T(8,128)} %shard_map.55.pack_ref), custom_call_target="tpu_custom_call" | custom-call | tf_op jit(solution)/shard_map/pallas_call | solution.py:370
  306.2 49.4 %shard_map.59 = (f32[1024,1024]{1,0:T(8,128)S(1)}, f32[4,256,256]{2,1,0:T(8,128)S(1)}) custom-call(f32[1024,1024]{1,0:T(8,128)} %bitcast.11), custom_call_target="tpu_custom_call" | custom-call | tf_op jit(solution)/shard_map/pallas_call | solution.py:527
  355.5 0.0 copy-start.3
  355.5 2.0 copy-done.3
  357.5 0.0 copy-start.4
  357.5 1.0 copy-done.4
  358.5 29.7 %shard_map.60 = f32[12,128,1536]{2,1,0:T(8,128)} custom-call(s32[11]{0:T(128)} %copy-done.5, f32[12,128,1536]{2,1,0:T(8,128)} %bitcast.9, f32[8,128,1536]{2,1,0:T(8,128)} %get-tuple-element.15.inc_ref, f32[11,128,1024]{2,1,0:T(8,128)} %get-tuple-element.16.panel_ref, f32[12,128,1024]{2,1,0:T(8,128)} %get-tuple-element.17.win_ref, f32[1024,1024]{1,0:T(8,128)} %copy-done.3, ...), custom_call_target="tpu_custom_call" | custom-call | tf_op jit(solution)/shard_map/pallas_call | solution.py:606
  (1 shorter events, 0.0 us)
Async XLA Ops:
  0.0 10.1 %copy-start.6 = (s32[1,4,1]{1,2,0:T(1,128)S(1)}, s32[1,4,1]{1,2,0:T(1,128)}, u32[]{:S(2)}) copy-start(s32[1,4,1]{1,2,0:T(1,128)} %param.8) | copy-start | bytes 52
  51.6 9.4 %copy-start.5 = (s32[11]{0:T(128)}, s32[11]{0:T(128)S(1)}, u32[]{:S(2)}) copy-start(s32[11]{0:T(128)S(1)} %pad_add_fusion.meta_ref) | copy-start | bytes 136
  51.6 3.7 copy-start
  55.3 2.8 copy-start.2
  61.1 2.5 copy-start.1
  355.5 2.0 copy-start.3
  357.5 1.0 copy-start.4

commit v2 on v1

--- a/solution.py
+++ b/solution.py
@@ -208,7 +208,7 @@
     )(front, packed, places)
 
 
-def second_exchange(panel_ref, pack_ref, own_ref, win_ref, inc_ref, ssend, srecv, wsend, wrecv, vsend, vrecv, asend, arecv, local):
+def second_exchange(panel_ref, pack_ref, a_ref, own_ref, win_ref, inc_ref, l_ref, i_ref, x_ref, ssend, srecv, wsend, wrecv, vsend, vrecv, asend, arecv, local):
     f = lax.axis_index("front")
     r = lax.axis_index("row")
     c = lax.axis_index("col")
@@ -296,7 +296,6 @@
         )
 
     keep_win = pltpu.make_async_copy(panel_ref.at[0], win_ref.at[lax.rem(r, 4)], local.at[0])
-    keep_own = pltpu.make_async_copy(panel_ref, own_ref, local.at[1])
     own_inc = pltpu.make_async_copy(pack_ref.at[f], inc_ref.at[f], local.at[2])
 
     @pl.when(c == 0)
@@ -318,7 +317,6 @@
         hand.start()
         for d in range(1, F):
             contrib_low(d).start()
-        keep_own.start()
 
     @pl.when(c == 1)
     def _():
@@ -326,6 +324,8 @@
             contrib_high(d).start()
 
     own_inc.start()
+
+    cholesky_body(a_ref, l_ref, i_ref, x_ref)
 
     @pl.when(c == 0)
     def _():
@@ -351,7 +351,6 @@
         hand.wait_send()
         for d in range(1, F):
             contrib_low(d).wait()
-        keep_own.wait()
 
     @pl.when(c == 1)
     def _():
@@ -366,17 +365,20 @@
     own_inc.wait()
 
 
-def exchange_two(panel, packed):
+def exchange_two(panel, packed, pivot):
     return pl.pallas_call(
         second_exchange,
         out_shape=(
             jax.ShapeDtypeStruct((LB - 1, B, PC), F32),
             jax.ShapeDtypeStruct((12, B, PC), F32),
             jax.ShapeDtypeStruct((F, B, HW), F32),
+            jax.ShapeDtypeStruct((PC, PC), F32),
+            jax.ShapeDtypeStruct((PC // KD, KD, KD), F32),
         ),
-        in_specs=[ANY] * 2,
-        out_specs=(ANY,) * 3,
+        in_specs=[ANY, ANY, VM],
+        out_specs=(ANY, ANY, ANY, VM, VM),
         scratch_shapes=[
+            pltpu.VMEM((NB, B, B), F32),
             pltpu.SemaphoreType.DMA,
             pltpu.SemaphoreType.DMA,
             pltpu.SemaphoreType.DMA((R,)),
@@ -387,8 +389,8 @@
             pltpu.SemaphoreType.DMA((F,)),
             pltpu.SemaphoreType.DMA((3,)),
         ],
-        compiler_params=pltpu.CompilerParams(collective_id=1, has_side_effects=True),
-    )(panel, packed)
+        compiler_params=pltpu.CompilerParams(collective_id=1, has_side_effects=True, vmem_limit_bytes=48 * MIB),
+    )(panel, packed, pivot)
 
 
 def assemble_kernel(meta_ref, front_ref, inc_ref, out_ref):
@@ -482,7 +484,7 @@
     return jnp.concatenate(factor, 0), jnp.concatenate(inverse, 0)
 
 
-def cholesky_kernel(a_ref, l_ref, i_ref, x_ref):
+def cholesky_body(a_ref, l_ref, i_ref, x_ref):
     l_ref[...] = a_ref[...]
     row_id = lax.broadcasted_iota(jnp.int32, (B, B), 0)
     col_id = lax.broadcasted_iota(jnp.int32, (B, B), 1)
@@ -523,21 +525,7 @@
         i_ref[i, B:, B:] = high
 
 
-def cholesky(a):
-    return pl.pallas_call(
-        cholesky_kernel,
-        out_shape=(
-            jax.ShapeDtypeStruct((PC, PC), F32),
-            jax.ShapeDtypeStruct((PC // KD, KD, KD), F32),
-        ),
-        in_specs=[VM],
-        out_specs=(VM, VM),
-        scratch_shapes=[pltpu.VMEM((NB, B, B), F32)],
-        compiler_params=pltpu.CompilerParams(vmem_limit_bytes=48 * MIB),
-    )(a)
-
-
-def final_kernel(meta_ref, front_ref, inc_ref, panel_ref, win_ref, l_ref, i_ref, out_ref, ph, plo, wh, wl, l3):
+def final_kernel(meta_ref, front_ref, inc_ref, panel_any, own_any, win_ref, l_ref, i_ref, out_ref, panel_ref, ph, plo, wh, wl, l3, sem):
     t = pl.program_id(0)
     col = meta_ref[1]
     steps = PC // KD
@@ -561,9 +549,18 @@
 
     @pl.when(t == 0)
     def _():
+        @pl.when(col == 0)
+        def _():
+            pltpu.make_async_copy(panel_any, panel_ref, sem).start()
+
+        @pl.when(col == 1)
+        def _():
+            pltpu.make_async_copy(own_any, panel_ref, sem).start()
+
         for m in range(steps - 1):
             hi, lo = split(l_ref[:, m * KD : (m + 1) * KD])
             l3[:, 3 * m * KD : 3 * (m + 1) * KD] = right3(hi, lo)
+        pltpu.make_async_copy(panel_any, panel_ref, sem).wait()
         solve(6, panel_ref, ph, plo, 0)
         solve(5, panel_ref, ph, plo, 6)
         solve(4, win_ref, wh, wl, 0)
@@ -600,7 +597,7 @@
                 out_ref[pl.ds(place, 1)] += inc_ref[s : s + 1]
 
 
-def final(meta, front, inc, panel, win, low, inv):
+def final(meta, front, inc, panel, own, win, low, inv):
     tiles = HW // KD
     whole = dict(pipeline_mode=pl.Buffered(1))
     return pl.pallas_call(
@@ -611,23 +608,26 @@
             in_specs=[
                 pl.BlockSpec((LB, B, KD), lambda t, meta: (0, 0, t)),
                 pl.BlockSpec((F, B, KD), lambda t, meta: (0, 0, t)),
-                pl.BlockSpec((LB - 1, B, PC), lambda t, meta: (0, 0, 0), **whole),
+                ANY,
+                ANY,
                 pl.BlockSpec((12, B, PC), lambda t, meta: (0, 0, 0), **whole),
                 pl.BlockSpec((PC, PC), lambda t, meta: (0, 0), **whole),
                 pl.BlockSpec((PC // KD, KD, KD), lambda t, meta: (0, 0, 0), **whole),
             ],
             out_specs=pl.BlockSpec((LB, B, KD), lambda t, meta: (0, 0, t)),
             scratch_shapes=[
+                pltpu.VMEM((LB - 1, B, PC), F32),
                 pltpu.VMEM(((LB - 1) * B, PC), jnp.bfloat16),
                 pltpu.VMEM(((LB - 1) * B, PC), jnp.bfloat16),
                 pltpu.VMEM((12 * B, PC), jnp.bfloat16),
                 pltpu.VMEM((12 * B, PC), jnp.bfloat16),
                 pltpu.VMEM((PC, 3 * (PC - KD)), jnp.bfloat16),
+                pltpu.SemaphoreType.DMA,
             ],
         ),
         out_shape=jax.ShapeDtypeStruct((LB, B, HW), F32),
         compiler_params=pltpu.CompilerParams(vmem_limit_bytes=60 * MIB),
-    )(meta, front, inc, panel, win, low, inv)
+    )(meta, front, inc, panel, own, win, low, inv)
 
 
 def on_device(front_matrix, front_sizes, contrib, dest_front, dest_local):
@@ -643,9 +643,8 @@
     row_col = jnp.stack([lax.axis_index("row"), lax.axis_index("col"), front_sizes[0]]).astype(jnp.int32)
     meta = jnp.concatenate([row_col, got[:, 0, 0]])
     panel = assemble(meta, front, inc)
-    own, win, inc_rest = exchange_two(panel, packed)
-    low, inv = cholesky(pivot.reshape(PC, PC))
-    out = final(meta, front, inc_rest, own, win, low, inv)
+    own, win, inc_rest, low, inv = exchange_two(panel, packed, pivot.reshape(PC, PC))
+    out = final(meta, front, inc_rest, panel, own, win, low, inv)
     return out[None]
 
 

time: 389 us -> 227 us (0.58)
  the two profiles are of different devices: /device:TPU:0 before, /device:TPU:25 now
where the time goes in v2:
time: 227 us; the launch traced here: 226 us
  Pallas kernels  209 us (92%)
  local copies, waits for them, and re-layouts  13.6 us (6%)
    pallas_call x1, Pallas kernels, exchange_two(): pl.pallas_call(second_exchange, out_shape=(jax.ShapeDtypeStruct((LB - 1,...  118 us
    pallas_call x1, Pallas kernels, final(): pl.pallas_call(final_kernel, grid_spec=pltpu.PrefetchScalarGridSpec(num_s...  40.6 us
    pallas_call x1, Pallas kernels, exchange_one(): pl.pallas_call(first_exchange, out_shape=(jax.ShapeDtypeStruct((R, B, PC)...  40.5 us
    unnamed x12, local copies, waits for them, and re-layouts  11.9 us
    pallas_call x1, Pallas kernels, pack(): pl.pallas_call(pack_kernel, grid_spec=pltpu.PrefetchScalarGridSpec(num_sc...  7.6 us

profile of v2, /device:TPU:25, one launch (start us, length us, event | category | flops | bytes accessed | tf_op | source)
XLA Modules:
  0.0 226.0 jit_solution(1889992784960964768)
XLA Ops:
  0.7 0.7 fusion
  1.4 1.3 select_reduce_fusion
  2.7 0.7 broadcast_in_dim.40.place_ref
  3.4 7.6 %shard_map.55.pack_ref = f32[8,128,1536]{2,1,0:T(8,128)} custom-call(s32[8]{0:T(128)} %get-tuple-element.22.which_ref, f32[4,128,1536]{2,1,0:T(8,128)} %bitcast.12), custom_call_target="tpu_custom_call" | custom-call | tf_op jit(solution)/shard_map/pallas_call | solution.py:60
  11.0 40.5 %shard_map.56 = (f32[8,128,1024]{2,1,0:T(8,128)}, f32[8,128,1536]{2,1,0:T(8,128)}, s32[8,8,128]{2,1,0:T(8,128)}) custom-call(f32[12,128,1536]{2,1,0:T(8,128)} %bitcast.8, f32[8,128,1536]{2,1,0:T(8,128)} %shard_map.55.pack_ref, s32[8,8,128]{2,1,0:T(8,128)} %broadcast_in_dim.40.place_ref), custom_call_target="tpu_custom_call" | custom-call | tf_op jit(solution)/shard_map/pallas_call | solution.py:188
  51.5 1.0 slice_reduce_fusion
  52.5 0.1 pad_add_fusion.meta_ref
  52.6 0.0 copy-start
  52.6 3.7 %copy-done = f32[1,12,128,1536]{3,2,1,0:T(8,128)S(1)} copy-done((f32[1,12,128,1536]{3,2,1,0:T(8,128)S(1)}, f32[1,12,128,1536]{3,2,1,0:T(8,128)}, u32[]{:S(2)}) %copy-start) | copy-done | bytes 9437208
  56.3 0.0 copy-start.2
  56.3 2.8 %copy-done.2 = f32[8,128,1536]{2,1,0:T(8,128)S(1)} copy-done((f32[8,128,1536]{2,1,0:T(8,128)S(1)}, f32[8,128,1536]{2,1,0:T(8,128)}, u32[]{:S(2)}) %copy-start.2) | copy-done | bytes 6291480
  59.1 0.0 copy-start.5
  59.1 3.0 %shard_map.57.panel_ref.panel_any = f32[11,128,1024]{2,1,0:T(8,128)S(1)} custom-call(s32[11]{0:T(128)S(1)} %pad_add_fusion.meta_ref, f32[12,128,1536]{2,1,0:T(8,128)S(1)} %bitcast.10, f32[8,128,1536]{2,1,0:T(8,128)S(1)} %copy-done.2), custom_call_target="tpu_custom_call" | custom-call | tf_op jit(solution)/shard_map/pallas_call | solution.py:407
  62.2 0.0 copy-done.5
  62.2 0.0 copy-start.1
  62.2 2.4 %copy-done.1 = f32[11,128,1024]{2,1,0:T(8,128)} copy-done((f32[11,128,1024]{2,1,0:T(8,128)}, f32[11,128,1024]{2,1,0:T(8,128)S(1)}, u32[]{:S(2)}) %copy-start.1) | copy-done | bytes 5767192
  64.6 117.6 %shard_map.58 = (f32[11,128,1024]{2,1,0:T(8,128)}, f32[12,128,1024]{2,1,0:T(8,128)}, f32[8,128,1536]{2,1,0:T(8,128)}, f32[1024,1024]{1,0:T(8,128)S(1)}, f32[4,256,256]{2,1,0:T(8,128)S(1)}) custom-call(f32[11,128,1024]{2,1,0:T(8,128)} %copy-done.1, f32[8,128,1536]{2,1,0:T(8,128)} %shard_map.55.pack_ref, f32[1024,1024]{1,0:T(8,128)} %bitcast.11), custom_call_target="tpu_custom_call" | custom-call | tf_op jit(solution)/shard_map/pallas_call | solution.py:369
  182.2 0.0 copy-start.3
  182.2 2.1 copy-done.3
  184.3 0.0 copy-start.4
  184.3 1.0 copy-done.4
  185.2 40.6 %shard_map.59 = f32[12,128,1536]{2,1,0:T(8,128)} custom-call(s32[11]{0:T(128)} %copy-done.5, f32[12,128,1536]{2,1,0:T(8,128)} %bitcast.9, f32[8,128,1536]{2,1,0:T(8,128)} %get-tuple-element.16.inc_ref, f32[11,128,1024]{2,1,0:T(8,128)} %copy-done.1, f32[11,128,1024]{2,1,0:T(8,128)} %get-tuple-element.17.own_any, f32[12,128,1024]{2,1,0:T(8,128)} %get-tuple-element.18.win_ref, ...), custom_call_target="tpu_custom_call" | custom-call | tf_op jit(solution)/shard_map/pallas_call | solution.py:603
  (1 shorter events, 0.0 us)
Async XLA Ops:
  52.6 3.7 %copy-start = (f32[1,12,128,1536]{3,2,1,0:T(8,128)S(1)}, f32[1,12,128,1536]{3,2,1,0:T(8,128)}, u32[]{:S(2)}) copy-start(f32[1,12,128,1536]{3,2,1,0:T(8,128)} %param.5) | copy-start | bytes 28311556
  56.3 2.8 %copy-start.2 = (f32[8,128,1536]{2,1,0:T(8,128)S(1)}, f32[8,128,1536]{2,1,0:T(8,128)}, u32[]{:S(2)}) copy-start(f32[8,128,1536]{2,1,0:T(8,128)} %get-tuple-element.14.inc_ref) | copy-start | bytes 18874372
  59.1 3.1 %copy-start.5 = (s32[11]{0:T(128)}, s32[11]{0:T(128)S(1)}, u32[]{:S(2)}) copy-start(s32[11]{0:T(128)S(1)} %pad_add_fusion.meta_ref) | copy-start | bytes 136
  62.2 2.4 %copy-start.1 = (f32[11,128,1024]{2,1,0:T(8,128)}, f32[11,128,1024]{2,1,0:T(8,128)S(1)}, u32[]{:S(2)}) copy-start(f32[11,128,1024]{2,1,0:T(8,128)S(1)} %shard_map.57.panel_ref.panel_any) | copy-start | bytes 17301508
  182.2 2.1 copy-start.3
  184.3 1.0 copy-start.4

commit v3 on v0

v3 whole, which is shorter than its diff:
```python
import functools

import jax
import jax.numpy as jnp
from jax import lax
from jax.experimental import pallas as pl
from jax.experimental.pallas import tpu as pltpu
from jax.sharding import PartitionSpec as P

F = 8
R = 8
B = 128
LB = 12
HW = 1536
PC = 1024
NB = PC // B
KD = 256
MESH = pl.DeviceIdType.MESH
ANY = pl.BlockSpec(memory_space=pl.ANY)
VM = pl.BlockSpec(memory_space=pltpu.VMEM)
F32 = jnp.float32
MIB = 2**20


def split(x):
    hi = x.astype(jnp.bfloat16)
    return hi, (x - hi.astype(F32)).astype(jnp.bfloat16)


def left3(hi, lo):
    return jnp.concatenate([hi, lo, hi], 1)


def right3(hi, lo):
    return jnp.concatenate([hi, hi, lo], 1)


def dot_nt(a, b):
    return lax.dot_general(a, b, (((1,), (1,)), ((), ())), preferred_element_type=F32)


def dot_nn(a, b):
    return lax.dot_general(a, b, (((1,), (0,)), ((), ())), preferred_element_type=F32)


def dot3(a, b):
    return dot_nt(left3(*split(a)), right3(*split(b)))


def dot3_nn(a, b):
    bh, bl = split(b)
    return dot_nn(left3(*split(a)), jnp.concatenate([bh, bh, bl], 0))


def recip(x):
    first = pl.reciprocal(x, approx=True)
    return first * (2.0 - x * first)


def lane_spread(x, k):
    return jnp.broadcast_to(x[:, k : k + 1], (8, B))


def row_spread(x, j):
    return jnp.broadcast_to(x[j : j + 1, :], (8, B))


def factor_block(sym):
    sub = lax.broadcasted_iota(jnp.int32, (8, B), 0)
    lane = lax.broadcasted_iota(jnp.int32, (8, B), 1)
    count = B // 8
    rows = [sym[q * 8 : (q + 1) * 8, :] for q in range(count)]
    eyes = [jnp.where(lane == sub + q * 8, 1.0, 0.0).astype(F32) for q in range(count)]
    factor, inverse = [], []
    for p in range(count):
        v, e = rows[p], eyes[p]
        c = [lane_spread(v, p * 8 + k) for k in range(8)]
        more = p < count - 1
        if more:
            v2, e2 = rows[p + 1], eyes[p + 1]
            c2 = [lane_spread(v2, p * 8 + k) for k in range(8)]
        diagonal = None
        for j in range(8):
            pivot = row_spread(c[j], j)
            diagonal = pivot if diagonal is None else jnp.where(sub == j, pivot, diagonal)
            over = recip(pivot)
            rv, re = row_spread(v, j), row_spread(e, j)
            m = jnp.where(sub > j, c[j] * over, 0.0)
            if more:
                m2 = c2[j] * over
            for k in range(j + 1, 8):
                s = row_spread(c[k], j)
                c[k] = c[k] - m * s
                if more:
                    c2[k] = c2[k] - m2 * s
            v = v - m * rv
            e = e - m * re
            if more:
                v2 = v2 - m2 * rv
                e2 = e2 - m2 * re
        scale = lax.rsqrt(diagonal)
        factor.append(jnp.where(lane >= sub + p * 8, v * scale, 0.0))
        inverse.append(e * scale)
        if more:
            rows[p + 1], eyes[p + 1] = v2, e2
        if p < count - 2:
            t = (v * recip(diagonal)).T
            rv = [row_spread(v, j) for j in range(8)]
            re = [row_spread(e, j) for j in range(8)]
            for q in range(p + 2, count):
                tq = t[q * 8 : (q + 1) * 8, :]
                for j in range(8):
                    m = jnp.broadcast_to(tq[:, j : j + 1], (8, B))
                    rows[q] = rows[q] - m * rv[j]
                    eyes[q] = eyes[q] - m * re[j]
    return jnp.concatenate(factor, 0), jnp.concatenate(inverse, 0)


def cholesky_body(a_ref, l_ref, i_ref, x_ref, after):
    for i in range(NB):
        l_ref[i * B : (i + 1) * B, : (i + 1) * B] = a_ref[i, :, : (i + 1) * B]
    row_id = lax.broadcasted_iota(jnp.int32, (B, B), 0)
    col_id = lax.broadcasted_iota(jnp.int32, (B, B), 1)

    def step(k, carry):
        o = pl.multiple_of(k * B, B)
        d = l_ref[pl.ds(o, B), pl.ds(o, B)]
        lt, li = factor_block(jnp.where(row_id >= col_id, d, d.T))
        l_ref[pl.ds(o, B), pl.ds(o, B)] = lt.T
        x_ref[k] = li

        def trailing(kk):
            def run():
                base = (kk + 1) * B
                x = dot3(l_ref[base:, kk * B : base], li)
                l_ref[base:, kk * B : base] = x
                xh, xl = split(x)
                xa, xb = left3(xh, xl), right3(xh, xl)
                for j in range(kk + 1, NB):
                    jo = (j - kk - 1) * B
                    l_ref[j * B :, j * B : (j + 1) * B] -= dot_nt(xa[jo:], xb[jo : jo + B])

            return run

        for kk in range(NB - 1):
            pl.when(k == kk)(trailing(kk))
        after(k)
        return carry

    lax.fori_loop(0, NB, step, 0)
    for i in range(NB - 1):
        l_ref[i * B : (i + 1) * B, (i + 1) * B :] = jnp.zeros((B, (NB - 1 - i) * B), F32)
    for i in range(NB // 2):
        low, high = x_ref[2 * i], x_ref[2 * i + 1]
        between = l_ref[(2 * i + 1) * B : (2 * i + 2) * B, 2 * i * B : (2 * i + 1) * B]
        i_ref[i, :B, :B] = low
        i_ref[i, :B, B:] = jnp.zeros((B, B), F32)
        i_ref[i, B:, :B] = -dot3_nn(high, dot3_nn(between, low))
        i_ref[i, B:, B:] = high


def exchange_kernel(
    front_ref, contrib_ref, dest_ref, local_ref, size_ref,
    panel_ref, win_ref, inc_ref, got_ref, l_ref, i_ref,
    x_ref, cont, packed, pan, inc_p, piv, place_v,
    psend, precv, fsend, asend, arecv, bsend, brecv, lsend, lrecv, hsend, hrecv, wsend, wrecv, gsend, local,
):
    f = lax.axis_index("front")
    r = lax.axis_index("row")
    c = lax.axis_index("col")
    y = lax.rem(r, 4)
    side = r - y
    across = lax.rem(r + 4, R)
    rest = HW - PC

    load_contrib = pltpu.make_async_copy(contrib_ref, cont, local.at[0])
    load_contrib.start()
    load_panel = pltpu.make_async_copy(front_ref.at[pl.ds(1, LB - 1), :, pl.ds(0, PC)], pan, local.at[1])

    @pl.when(c == 0)
    def _():
        load_panel.start()

    barrier = pltpu.get_barrier_semaphore()
    for d in range(1, F):
        pl.semaphore_signal(barrier, inc=1, device_id={"front": lax.rem(f + d, F)}, device_id_type=MESH)
        pl.semaphore_signal(barrier, inc=1, device_id={"row": lax.rem(r + d, R)}, device_id_type=MESH)
    for d in range(R):
        pl.semaphore_signal(barrier, inc=1, device_id={"row": lax.rem(r + d, R), "col": 1 - c}, device_id_type=MESH)
    pl.semaphore_wait(barrier, F - 1 + R - 1 + R)

    def send(src, dst, send_sem, recv_sem, **device):
        return pltpu.make_async_remote_copy(
            src_ref=src, dst_ref=dst, send_sem=send_sem, recv_sem=recv_sem, device_id=device, device_id_type=MESH
        )

    def pivot_copy(i, d):
        cols = pl.ds(0, (i + 1) * B)
        return send(front_ref.at[0, :, cols], piv.at[i, :, cols], psend.at[d], precv.at[i], row=lax.rem(r + d, R))

    def pivot_own(i):
        cols = pl.ds(0, (i + 1) * B)
        return pltpu.make_async_copy(front_ref.at[0, :, cols], piv.at[i, :, cols], local.at[2])

    def pivot_hand(i, own):
        cols = pl.ds(0, (i + 1) * B)
        src = front_ref.at[0, :, cols] if own else piv.at[i, :, cols]
        return send(src, piv.at[i, :, cols], fsend.at[i], precv.at[i], col=1)

    @pl.when(c == 0)
    def _():
        for i in range(R):
            @pl.when(r == i)
            def _():
                for d in range(1, R):
                    pivot_copy(i, d).start()
                pivot_hand(i, True).start()
                pivot_own(i).start()

    def contrib_panel(d):
        to = lax.rem(f + d, F)
        return send(packed.at[to, :, pl.ds(0, PC)], inc_p.at[f], asend.at[d], arecv.at[d], front=to)

    def contrib_low(d):
        to = lax.rem(f + d, F)
        cols = pl.ds(PC, rest)
        return send(packed.at[to, :, cols], inc_ref.at[f, :, cols], bsend.at[d], brecv.at[d], front=to)

    def contrib_high(d):
        to = lax.rem(f + d, F)
        return send(packed.at[to], inc_ref.at[f], bsend.at[d], brecv.at[d], front=to)

    def place_copy(d):
        to = lax.rem(f + d, F)
        return send(place_v.at[to], got_ref.at[f], lsend.at[d], lrecv.at[d], front=to)

    def choice(to):
        which, place = 0, -1
        for k in range(4):
            mine = dest_ref[k] == to
            which = jnp.where(mine, k, which)
            place = jnp.where(mine, local_ref[k], place)
        return which, place

    load_contrib.wait()

    @pl.when(c == 0)
    def _():
        def one(d, carry):
            to = lax.rem(f + d, F)
            which, _ = choice(to)
            packed[to, :, :PC] = cont[which, :, :PC]
            contrib_panel(d).start()
            return carry

        lax.fori_loop(1, F, one, 0)
        which, _ = choice(f)
        inc_p[f] = cont[which, :, :PC]

    def place_one(d, carry):
        to = lax.rem(f + d, F)
        _, place = choice(to)
        place_v[to] = jnp.full((8, B), place, jnp.int32)
        place_copy(d).start()
        return carry

    lax.fori_loop(1, F, place_one, 0)
    _, own_place = choice(f)
    got_ref[f] = jnp.full((8, B), own_place, jnp.int32)

    def pack_low(d, carry):
        to = lax.rem(f + d, F)
        which, _ = choice(to)
        packed[to, :, PC:] = cont[which, :, PC:]
        return carry

    def pack_high(d, carry):
        to = lax.rem(f + d, F)
        which, _ = choice(to)
        packed[to] = cont[which]
        return carry

    @pl.when(c == 0)
    def _():
        lax.fori_loop(0, F, pack_low, 0)

    @pl.when(c == 1)
    def _():
        lax.fori_loop(0, F, pack_high, 0)

    inc_own_low = pltpu.make_async_copy(packed.at[f, :, pl.ds(PC, rest)], inc_ref.at[f, :, pl.ds(PC, rest)], local.at[3])
    inc_own_high = pltpu.make_async_copy(packed.at[f], inc_ref.at[f], local.at[3])

    for d in range(1, F):
        place_copy(d).wait()

    @pl.when(c == 0)
    def _():
        for d in range(R):
            for i in range(R):
                @pl.when(lax.rem(r + d, R) == i)
                def _():
                    if d > 0:
                        pivot_hand(i, False).wait_recv()
                        pivot_hand(i, False).start()
                    else:
                        pivot_own(i).wait()

    @pl.when(c == 1)
    def _():
        for i in range(R):
            pivot_hand(i, False).wait_recv()

    near = (1, 3, 2)

    def row_at(d):
        return side + lax.rem(y + d, 4)

    def own_second(n):
        src, dst = pan.at[1], win_ref.at[4 + r]
        if n == 0:
            return send(src, dst, wsend.at[0], wrecv.at[4 + r], row=across, col=1)
        if n == 1:
            return send(src, dst, wsend.at[1], wrecv.at[4 + r], col=1)
        return send(src, dst, wsend.at[n], wrecv.at[4 + r], row=row_at(near[n - 2]), col=1)

    def own_high(n):
        src, dst, rs = pan.at[0], win_ref.at[r - 4], wrecv.at[r - 4]
        if n == 0:
            return send(src, dst, wsend.at[5], rs, row=across, col=1)
        if n == 1:
            return send(src, dst, wsend.at[6], rs, col=1)
        return send(src, dst, wsend.at[5 + n], rs, row=row_at(near[n - 2]), col=1)

    def own_low(n):
        src, dst, rs = pan.at[0], win_ref.at[r], wrecv.at[r]
        if n == 0:
            return send(src, dst, wsend.at[5], rs, row=across)
        return send(src, dst, wsend.at[6 + n], rs, row=row_at(near[n - 1]))

    keep_low = pltpu.make_async_copy(pan.at[0], win_ref.at[y], local.at[4])
    keep_panel = pltpu.make_async_copy(pan, panel_ref, local.at[5])
    hand = send(pan, panel_ref, hsend, hrecv, col=1)

    def landed(i):
        return send(pan.at[0], win_ref.at[i], gsend.at[0], wrecv.at[i], col=1 - c)

    def pass_second(n):
        at = 4 + across
        return send(win_ref.at[at], win_ref.at[at], gsend.at[n], wrecv.at[at], row=row_at(near[n]))

    def pass_first(n):
        return send(win_ref.at[y], win_ref.at[y], gsend.at[3 + n], wrecv.at[y], row=row_at(near[n]))

    def assemble(lb):
        valid = (lb * R + r) * B < size_ref[0]

        def eight(i, carry):
            at = pl.ds(pl.multiple_of(i * 8, 8), 8)
            total = jnp.where(valid, pan[lb - 1, at, :], 0.0)
            for s in range(F):
                mask = jnp.concatenate([got_ref[s]] * (PC // B), 1) == lb
                total = total + jnp.where(mask, inc_p[s, at, :], 0.0)
            pan[lb - 1, at, :] = total
            return carry

        lax.fori_loop(0, B // 8, eight, 0)

    def after(k):
        @pl.when((k == 1) & (c == 0))
        def _():
            load_panel.wait()
            for d in range(1, F):
                contrib_panel(d).wait()
            assemble(2)
            for n in range(5):
                own_second(n).start()
            assemble(1)

            @pl.when(r >= 4)
            def _():
                for n in range(5):
                    own_high(n).start()

            @pl.when(r < 4)
            def _():
                for n in range(4):
                    own_low(n).start()
                keep_low.start()

            for d in range(1, F):
                contrib_low(d).start()
            inc_own_low.start()

            def others(lb, carry):
                assemble(lb)
                return carry

            lax.fori_loop(3, LB, others, 0)
            hand.start()
            keep_panel.start()

        @pl.when((k == 1) & (c == 1))
        def _():
            for d in range(1, F):
                contrib_high(d).start()
            inc_own_high.start()

        @pl.when((k == 3) & (c == 0) & (r >= 4))
        def _():
            landed(y).wait_recv()
            for n in range(3):
                pass_first(n).start()

        @pl.when((k == 3) & (c == 1))
        def _():
            landed(4 + across).wait_recv()
            for n in range(3):
                pass_second(n).start()

            @pl.when(r < 4)
            def _():
                landed(y).wait_recv()
                for n in range(3):
                    pass_first(n).start()

    cholesky_body(piv, l_ref, i_ref, x_ref, after)

    @pl.when(c == 0)
    def _():
        for i in range(R):
            @pl.when(r == i)
            def _():
                for d in range(1, R):
                    pivot_copy(i, d).wait_send()
            pivot_hand(i, False).wait_send()
        for n in range(5):
            own_second(n).wait_send()

        @pl.when(r >= 4)
        def _():
            for n in range(5):
                own_high(n).wait_send()
            for n in range(3):
                pass_first(n).wait_send()

        @pl.when(r < 4)
        def _():
            for n in range(4):
                own_low(n).wait_send()
            keep_low.wait()

        for i in range(4):
            @pl.when(y != i)
            def _():
                landed(i).wait_recv()

        hand.wait_send()
        keep_panel.wait()
        for d in range(1, F):
            contrib_low(d).wait()
        inc_own_low.wait()

    @pl.when(c == 1)
    def _():
        hand.wait_recv()
        for i in range(4):
            @pl.when((y != i) | (r >= 4))
            def _():
                landed(i).wait_recv()
        for q in range(R):
            @pl.when(across != q)
            def _():
                landed(4 + q).wait_recv()
        for n in range(3):
            pass_second(n).wait_send()

        @pl.when(r < 4)
        def _():
            for n in range(3):
                pass_first(n).wait_send()

        for d in range(1, F):
            contrib_high(d).wait()
        inc_own_high.wait()


def exchange(front, contrib, dest, place, size):
    sm = pl.BlockSpec(memory_space=pltpu.SMEM)
    eight = pltpu.SemaphoreType.DMA((8,))
    one = pltpu.SemaphoreType.DMA
    return pl.pallas_call(
        exchange_kernel,
        out_shape=(
            jax.ShapeDtypeStruct((LB - 1, B, PC), F32),
            jax.ShapeDtypeStruct((12, B, PC), F32),
            jax.ShapeDtypeStruct((F, B, HW), F32),
            jax.ShapeDtypeStruct((F, 8, B), jnp.int32),
            jax.ShapeDtypeStruct((PC, PC), F32),
            jax.ShapeDtypeStruct((PC // KD, KD, KD), F32),
        ),
        in_specs=[ANY, ANY, sm, sm, sm],
        out_specs=(ANY, ANY, ANY, VM, VM, VM),
        scratch_shapes=[
            pltpu.VMEM((NB, B, B), F32),
            pltpu.VMEM((4, B, HW), F32),
            pltpu.VMEM((F, B, HW), F32),
            pltpu.VMEM((LB - 1, B, PC), F32),
            pltpu.VMEM((F, B, PC), F32),
            pltpu.VMEM((R, B, PC), F32),
            pltpu.VMEM((F, 8, B), jnp.int32),
            eight, eight, eight, eight, eight, eight, eight, eight, eight, one, one,
            pltpu.SemaphoreType.DMA((10,)),
            pltpu.SemaphoreType.DMA((12,)),
            pltpu.SemaphoreType.DMA((6,)),
            pltpu.SemaphoreType.DMA((6,)),
        ],
        compiler_params=pltpu.CompilerParams(collective_id=0, has_side_effects=True, vmem_limit_bytes=50 * MIB),
    )(front, contrib, dest, place, size)


def final_kernel(meta_ref, front_ref, inc_ref, panel_any, win_ref, l_ref, i_ref, out_ref, panel_ref, ph, plo, wh, wl, l3, sem):
    t = pl.program_id(0)
    col = meta_ref[1]
    steps = PC // KD

    def solve(blocks, source_ref, hi_ref, lo_ref, at):
        rows = blocks * B
        his, los = [], []
        for k in range(steps):
            cols = slice(k * KD, (k + 1) * KD)
            a = source_ref[pl.ds(at, blocks), :, cols].reshape(rows, KD)
            for m in range(k):
                a = a - dot_nt(
                    left3(his[m], los[m]), l3[cols, 3 * m * KD : 3 * (m + 1) * KD]
                )
            p = dot3(a, i_ref[k])
            hi, lo = split(p)
            his.append(hi)
            los.append(lo)
            hi_ref[pl.ds(at * B, rows), cols] = hi
            lo_ref[pl.ds(at * B, rows), cols] = lo

    @pl.when(t == 0)
    def _():
        pltpu.make_async_copy(panel_any, panel_ref, sem).start()

        for m in range(steps - 1):
            hi, lo = split(l_ref[:, m * KD : (m + 1) * KD])
            l3[:, 3 * m * KD : 3 * (m + 1) * KD] = right3(hi, lo)
        pltpu.make_async_copy(panel_any, panel_ref, sem).wait()
        solve(6, panel_ref, ph, plo, 0)
        solve(5, panel_ref, ph, plo, 6)
        solve(4, win_ref, wh, wl, 0)

        @pl.when(col == 1)
        def _():
            solve(4, win_ref, wh, wl, 4)
            solve(4, win_ref, wh, wl, 8)

    @pl.when((col == 0) & (t < steps))
    def _():
        row = pl.multiple_of(meta_ref[0] * B, B)
        for k in range(steps):
            @pl.when(t == k)
            def _():
                cols = slice(k * KD, (k + 1) * KD)
                out_ref[0] = l_ref[pl.ds(row, B), cols]
                out_ref[1:] = (ph[:, cols].astype(F32) + plo[:, cols].astype(F32)).reshape(LB - 1, B, KD)

    @pl.when((col == 1) | (t >= steps))
    def _():
        start = pl.multiple_of((t - jnp.where(col == 0, steps, 0)) * KD, KD)
        w_hi, w_lo = wh[pl.ds(start, KD), :], wl[pl.ds(start, KD), :]
        update = dot_nt(ph[...], w_hi) + dot_nt(plo[...], w_hi) + dot_nt(ph[...], w_lo)
        out_ref[0] = jnp.zeros((B, KD), F32)
        for lb in range(1, LB):
            valid = (lb * R + meta_ref[0]) * B < meta_ref[2]
            out_ref[lb] = jnp.where(valid, front_ref[lb], 0.0) - update[(lb - 1) * B : lb * B]
        for s in range(F):
            place = meta_ref[3 + s]

            @pl.when(place >= 0)
            def _():
                out_ref[pl.ds(place, 1)] += inc_ref[s : s + 1]


def final(meta, front, inc, panel, win, low, inv):
    tiles = HW // KD
    whole = dict(pipeline_mode=pl.Buffered(1))
    return pl.pallas_call(
        final_kernel,
        grid_spec=pltpu.PrefetchScalarGridSpec(
            num_scalar_prefetch=1,
            grid=(tiles,),
            in_specs=[
                pl.BlockSpec((LB, B, KD), lambda t, meta: (0, 0, t)),
                pl.BlockSpec((F, B, KD), lambda t, meta: (0, 0, t)),
                ANY,
                pl.BlockSpec((12, B, PC), lambda t, meta: (0, 0, 0), **whole),
                pl.BlockSpec((PC, PC), lambda t, meta: (0, 0), **whole),
                pl.BlockSpec((PC // KD, KD, KD), lambda t, meta: (0, 0, 0), **whole),
            ],
            out_specs=pl.BlockSpec((LB, B, KD), lambda t, meta: (0, 0, t)),
            scratch_shapes=[
                pltpu.VMEM((LB - 1, B, PC), F32),
                pltpu.VMEM(((LB - 1) * B, PC), jnp.bfloat16),
                pltpu.VMEM(((LB - 1) * B, PC), jnp.bfloat16),
                pltpu.VMEM((12 * B, PC), jnp.bfloat16),
                pltpu.VMEM((12 * B, PC), jnp.bfloat16),
                pltpu.VMEM((PC, 3 * (PC - KD)), jnp.bfloat16),
                pltpu.SemaphoreType.DMA,
            ],
        ),
        out_shape=jax.ShapeDtypeStruct((LB, B, HW), F32),
        compiler_params=pltpu.CompilerParams(vmem_limit_bytes=60 * MIB),
    )(meta, front, inc, panel, win, low, inv)


def on_device(front_matrix, front_sizes, contrib, dest_front, dest_local):
    front = front_matrix[0]
    panel, win, inc, got, low, inv = exchange(front, contrib[0], dest_front[0, :, 0], dest_local[0, :, 0], front_sizes)
    row_col = jnp.stack([lax.axis_index("row"), lax.axis_index("col"), front_sizes[0]]).astype(jnp.int32)
    meta = jnp.concatenate([row_col, got[:, 0, 0]])
    out = final(meta, front, inc, panel, win, low, inv)
    return out[None]


def solution(mesh):
    return jax.shard_map(
        on_device,
        mesh=mesh,
        in_specs=(
            P("front", None, "row", "col"),
            P("front"),
            P("front", None, "row", "col"),
            P("front", None, "row"),
            P("front", None, "row"),
        ),
        out_specs=P("front", None, "row", "col"),
        check_vma=False,
    )
```

time: 802 us -> 181 us (0.23)
  the two profiles are of different devices: /device:TPU:1 before, /device:TPU:31 now
where the time goes in v3:
time: 181 us
  Pallas kernels  177 us (98%)
  local copies, waits for them, and re-layouts  2.53 us (1%)
    pallas_call x1, Pallas kernels, exchange(): pl.pallas_call(exchange_kernel, out_shape=(jax.ShapeDtypeStruct((LB - 1,...  136 us
    pallas_call x1, Pallas kernels, final(): pl.pallas_call(final_kernel, grid_spec=pltpu.PrefetchScalarGridSpec(num_s...  40.7 us

profile of v3, /device:TPU:31, one launch (start us, length us, event | category | flops | bytes accessed | tf_op | source)
XLA Modules:
  0.0 180.7 jit_solution(17071146620600373353)
XLA Ops:
  0.7 0.0 copy-start.1
  0.7 0.6 copy-done.1
  1.3 0.0 copy-start.2
  1.3 0.7 copy-done.2
  2.0 136.0 %shard_map.55 = (f32[11,128,1024]{2,1,0:T(8,128)}, f32[12,128,1024]{2,1,0:T(8,128)}, f32[8,128,1536]{2,1,0:T(8,128)}, s32[8,8,128]{2,1,0:T(8,128)S(1)}, f32[1024...) custom-call(f32[12,128,1536]{2,1,0:T(8,128)} %bitcast.9, f32[4,128,1536]{2,1,0:T(8,128)} %bitcast.11, s32[4]{0:T(128)S(1)} %bitcast.7, ...), custom_call_target="tpu_custom_call" | custom-call | tf_op jit(solution)/shard_map/pallas_call | solution.py:492
  138.0 0.0 copy-start
  138.0 1.0 copy-done
  139.0 0.2 slice_reduce_fusion
  139.2 0.7 pad_add_fusion.meta_ref
  139.9 40.7 %shard_map.56 = f32[12,128,1536]{2,1,0:T(8,128)} custom-call(s32[11]{0:T(128)} %pad_add_fusion.meta_ref, f32[12,128,1536]{2,1,0:T(8,128)} %bitcast.10, f32[8,128,1536]{2,1,0:T(8,128)} %get-tuple-element.12.inc_ref, f32[11,128,1024]{2,1,0:T(8,128)} %get-tuple-element.13.panel_any, f32[12,128,1024]{2,1,0:T(8,128)} %get-tuple-element.14.win_ref, ...), custom_call_target="tpu_custom_call" | custom-call | tf_op jit(solution)/shard_map/pallas_call | solution.py:591
Async XLA Ops:
  0.7 0.7 copy-start.1
  1.3 0.7 copy-start.2
  138.0 1.0 copy-start

commit v4 on v3

v4 whole, which is shorter than its diff:
```python
import functools

import jax
import jax.numpy as jnp
from jax import lax
from jax.experimental import pallas as pl
from jax.experimental.pallas import tpu as pltpu
from jax.sharding import PartitionSpec as P

F = 8
R = 8
B = 128
LB = 12
HW = 1536
PC = 1024
NB = PC // B
PW = 512
KD = 256
KA = (1, 3)
KC = 0
KF = (3, 6)
MESH = pl.DeviceIdType.MESH
ANY = pl.BlockSpec(memory_space=pl.ANY)
VM = pl.BlockSpec(memory_space=pltpu.VMEM)
F32 = jnp.float32
BF16 = jnp.bfloat16
MIB = 2**20


def split(x):
    hi = x.astype(jnp.bfloat16)
    return hi, (x - hi.astype(F32)).astype(jnp.bfloat16)


def left3(hi, lo):
    return jnp.concatenate([hi, lo, hi], 1)


def right3(hi, lo):
    return jnp.concatenate([hi, hi, lo], 1)


def dot_nt(a, b):
    return lax.dot_general(a, b, (((1,), (1,)), ((), ())), preferred_element_type=F32)


def dot_nn(a, b):
    return lax.dot_general(a, b, (((1,), (0,)), ((), ())), preferred_element_type=F32)


def dot3(a, b):
    return dot_nt(left3(*split(a)), right3(*split(b)))


def dot3_nn(a, b):
    bh, bl = split(b)
    return dot_nn(left3(*split(a)), jnp.concatenate([bh, bh, bl], 0))


def recip(x):
    first = pl.reciprocal(x, approx=True)
    return first * (2.0 - x * first)


def lane_spread(x, k):
    return jnp.broadcast_to(x[:, k : k + 1], (8, B))


def row_spread(x, j):
    return jnp.broadcast_to(x[j : j + 1, :], (8, B))


def factor_block(sym):
    sub = lax.broadcasted_iota(jnp.int32, (8, B), 0)
    lane = lax.broadcasted_iota(jnp.int32, (8, B), 1)
    count = B // 8
    rows = [sym[q * 8 : (q + 1) * 8, :] for q in range(count)]
    eyes = [jnp.where(lane == sub + q * 8, 1.0, 0.0).astype(F32) for q in range(count)]
    factor, inverse = [], []
    for p in range(count):
        v, e = rows[p], eyes[p]
        c = [lane_spread(v, p * 8 + k) for k in range(8)]
        more = p < count - 1
        if more:
            v2, e2 = rows[p + 1], eyes[p + 1]
            c2 = [lane_spread(v2, p * 8 + k) for k in range(8)]
        diagonal = None
        for j in range(8):
            pivot = row_spread(c[j], j)
            diagonal = pivot if diagonal is None else jnp.where(sub == j, pivot, diagonal)
            over = recip(pivot)
            rv, re = row_spread(v, j), row_spread(e, j)
            m = jnp.where(sub > j, c[j] * over, 0.0)
            if more:
                m2 = c2[j] * over
            for k in range(j + 1, 8):
                s = row_spread(c[k], j)
                c[k] = c[k] - m * s
                if more:
                    c2[k] = c2[k] - m2 * s
            v = v - m * rv
            e = e - m * re
            if more:
                v2 = v2 - m2 * rv
                e2 = e2 - m2 * re
        scale = lax.rsqrt(diagonal)
        factor.append(jnp.where(lane >= sub + p * 8, v * scale, 0.0))
        inverse.append(e * scale)
        if more:
            rows[p + 1], eyes[p + 1] = v2, e2
        if p < count - 2:
            t = (v * recip(diagonal)).T
            rv = [row_spread(v, j) for j in range(8)]
            re = [row_spread(e, j) for j in range(8)]
            for q in range(p + 2, count):
                tq = t[q * 8 : (q + 1) * 8, :]
                for j in range(8):
                    m = jnp.broadcast_to(tq[:, j : j + 1], (8, B))
                    rows[q] = rows[q] - m * rv[j]
                    eyes[q] = eyes[q] - m * re[j]
    return jnp.concatenate(factor, 0), jnp.concatenate(inverse, 0)


def cholesky_body(a_ref, l_ref, i_ref, x_ref, lh, ll, after):
    row_id = lax.broadcasted_iota(jnp.int32, (B, B), 0)
    col_id = lax.broadcasted_iota(jnp.int32, (B, B), 1)

    def step(k, carry):
        def owed(kk):
            def run():
                o = kk * B
                a = a_ref[kk:, :, o : o + B].reshape(PC - o, B)
                if kk > 0:
                    mine_h, mine_l = lh[o : o + B, :o], ll[o : o + B, :o]
                    a = a - (dot_nt(lh[o:, :o], mine_h) + dot_nt(ll[o:, :o], mine_h) + dot_nt(lh[o:, :o], mine_l))
                l_ref[o:, o : o + B] = a

            return run

        for kk in range(NB):
            pl.when(k == kk)(owed(kk))
        o = pl.multiple_of(k * B, B)
        d = l_ref[pl.ds(o, B), pl.ds(o, B)]
        lt, li = factor_block(jnp.where(row_id >= col_id, d, d.T))
        l_ref[pl.ds(o, B), pl.ds(o, B)] = lt.T
        x_ref[k] = li

        def below(kk):
            def run():
                base = (kk + 1) * B
                x = dot3(l_ref[base:, kk * B : base], li)
                l_ref[base:, kk * B : base] = x
                lh[base:, kk * B : base], ll[base:, kk * B : base] = split(x)

            return run

        for kk in range(NB - 1):
            pl.when(k == kk)(below(kk))
        after(k)
        return carry

    lax.fori_loop(0, NB, step, 0)
    for i in range(NB - 1):
        l_ref[i * B : (i + 1) * B, (i + 1) * B :] = jnp.zeros((B, (NB - 1 - i) * B), F32)
    for i in range(NB // 2):
        low, high = x_ref[2 * i], x_ref[2 * i + 1]
        between = l_ref[(2 * i + 1) * B : (2 * i + 2) * B, 2 * i * B : (2 * i + 1) * B]
        i_ref[i, :B, :B] = low
        i_ref[i, :B, B:] = jnp.zeros((B, B), F32)
        i_ref[i, B:, :B] = -dot3_nn(high, dot3_nn(between, low))
        i_ref[i, B:, B:] = high


def exchange_kernel(
    front_ref, contrib_ref, dest_ref, local_ref, size_ref,
    ph_ref, plo_ref, wh_ref, wl_ref, inc_ref, got_ref, l_ref,
    i_ref, x_ref, lh, ll, cont, packed, pan, win_ref, inc_p, piv, place_v, ph, plo, wh, wl,
    psend, precv, fsend, qsend, qrecv, rsend, asend, arecv, bsend, brecv, lsend, lrecv, hsend, hrecv, wsend, wrecv, gsend, local, outs,
):
    f = lax.axis_index("front")
    r = lax.axis_index("row")
    c = lax.axis_index("col")
    y = lax.rem(r, 4)
    side = r - y
    across = lax.rem(r + 4, R)
    rest = HW - PC

    load_contrib = pltpu.make_async_copy(contrib_ref, cont, local.at[0])
    load_contrib.start()
    load_panel = pltpu.make_async_copy(front_ref.at[pl.ds(1, LB - 1), :, pl.ds(0, PC)], pan, local.at[1])

    @pl.when(c == 0)
    def _():
        load_panel.start()

    barrier = pltpu.get_barrier_semaphore()
    for d in range(1, F):
        pl.semaphore_signal(barrier, inc=1, device_id={"front": lax.rem(f + d, F)}, device_id_type=MESH)
        pl.semaphore_signal(barrier, inc=1, device_id={"row": lax.rem(r + d, R)}, device_id_type=MESH)
    for d in range(R):
        pl.semaphore_signal(barrier, inc=1, device_id={"row": lax.rem(r + d, R), "col": 1 - c}, device_id_type=MESH)
    pl.semaphore_wait(barrier, F - 1 + R - 1 + R)

    def send(src, dst, send_sem, recv_sem, **device):
        return pltpu.make_async_remote_copy(
            src_ref=src, dst_ref=dst, send_sem=send_sem, recv_sem=recv_sem, device_id=device, device_id_type=MESH
        )

    near = (1, 3, 2)

    def row_at(d):
        return side + lax.rem(y + d, 4)

    def part(i, late):
        return pl.ds(KD, (i - 1) * B) if late else pl.ds(0, KD)

    def pivot_copy(i, n, late):
        cols = part(i, late)
        ss, rs = (qsend, qrecv) if late else (psend, precv)
        row = across if n == 0 else row_at(near[n - 1])
        return send(front_ref.at[0, :, cols], piv.at[i, :, cols], ss.at[n], rs.at[i], row=row)

    def pivot_pass(i, n, late):
        cols = part(i, late)
        ss, rs = (qsend, qrecv) if late else (psend, precv)
        return send(piv.at[i, :, cols], piv.at[i, :, cols], ss.at[4 + n], rs.at[i], row=row_at(near[n]))

    def pivot_own(i):
        cols = pl.ds(0, max(i + 1, 2) * B)
        return pltpu.make_async_copy(front_ref.at[0, :, cols], piv.at[i, :, cols], local.at[2])

    def pivot_hand(i, own, late):
        cols = part(i, late)
        ss, rs = (rsend, qrecv) if late else (fsend, precv)
        src = front_ref.at[0, :, cols] if own else piv.at[i, :, cols]
        return send(src, piv.at[i, :, cols], ss.at[i], rs.at[i], col=1)

    @pl.when(c == 0)
    def _():
        for late in (False, True):
            for i in range(2 if late else 0, R):
                @pl.when(r == i)
                def _():
                    for n in range(4):
                        pivot_copy(i, n, late).start()
                    pivot_hand(i, True, late).start()
                    if not late:
                        pivot_own(i).start()

    def hand_on(late):
        order = [across] + [row_at(d) for d in near] + [(4 - side) + lax.rem(y + d, 4) for d in near]
        for at, row in enumerate(order):
            for i in range(2 if late else 0, R):
                @pl.when(row == i)
                def _():
                    pivot_hand(i, False, late).wait_recv()
                    if at == 0:
                        for n in range(3):
                            pivot_pass(i, n, late).start()
                    pivot_hand(i, False, late).start()

    def contrib_panel(d, h):
        to = lax.rem(f + d, F)
        cols = pl.ds(h * PW, PW)
        return send(packed.at[to, :, cols], inc_p.at[f, :, cols], asend.at[h, d], arecv.at[h, d], front=to)

    def contrib_low(d):
        to = lax.rem(f + d, F)
        cols = pl.ds(PC, rest)
        return send(packed.at[to, :, cols], inc_ref.at[f, :, cols], bsend.at[d], brecv.at[d], front=to)

    def contrib_high(d):
        to = lax.rem(f + d, F)
        return send(packed.at[to], inc_ref.at[f], bsend.at[d], brecv.at[d], front=to)

    def place_copy(d):
        to = lax.rem(f + d, F)
        return send(place_v.at[to], got_ref.at[f], lsend.at[d], lrecv.at[d], front=to)

    def choice(to):
        which, place = 0, -1
        for k in range(4):
            mine = dest_ref[k] == to
            which = jnp.where(mine, k, which)
            place = jnp.where(mine, local_ref[k], place)
        return which, place

    load_contrib.wait()

    @pl.when(c == 0)
    def _():
        def one(d, carry):
            to = lax.rem(f + d, F)
            which, _ = choice(to)
            packed[to, :, :PC] = cont[which, :, :PC]
            contrib_panel(d, 0).start()
            return carry

        lax.fori_loop(1, F, one, 0)
        for d in range(1, F):
            contrib_panel(d, 1).start()
        which, _ = choice(f)
        inc_p[f] = cont[which, :, :PC]

    def place_one(d, carry):
        to = lax.rem(f + d, F)
        _, place = choice(to)
        place_v[to] = jnp.full((8, B), place, jnp.int32)
        place_copy(d).start()
        return carry

    lax.fori_loop(1, F, place_one, 0)
    _, own_place = choice(f)
    got_ref[f] = jnp.full((8, B), own_place, jnp.int32)

    def pack_low(d, carry):
        to = lax.rem(f + d, F)
        which, _ = choice(to)
        packed[to, :, PC:] = cont[which, :, PC:]
        return carry

    def pack_high(d, carry):
        to = lax.rem(f + d, F)
        which, _ = choice(to)
        packed[to] = cont[which]
        return carry

    @pl.when(c == 0)
    def _():
        lax.fori_loop(0, F, pack_low, 0)

    @pl.when(c == 1)
    def _():
        lax.fori_loop(0, F, pack_high, 0)

    inc_own_low = pltpu.make_async_copy(packed.at[f, :, pl.ds(PC, rest)], inc_ref.at[f, :, pl.ds(PC, rest)], local.at[3])
    inc_own_high = pltpu.make_async_copy(packed.at[f], inc_ref.at[f], local.at[3])

    for d in range(1, F):
        place_copy(d).wait()

    @pl.when(c == 0)
    def _():
        hand_on(False)
        for i in range(R):
            @pl.when(r == i)
            def _():
                pivot_own(i).wait()

    @pl.when(c == 1)
    def _():
        for i in range(R):
            pivot_hand(i, False, False).wait_recv()

    def half_of(h):
        return pl.ds(h * PW, PW)

    def own_second(n, h):
        cols = half_of(h)
        src, dst, ss, rs = pan.at[1, :, cols], win_ref.at[4 + r, :, cols], wsend.at[h, n], wrecv.at[h, 4 + r]
        if n == 0:
            return send(src, dst, ss, rs, row=across, col=1)
        if n == 1:
            return send(src, dst, ss, rs, col=1)
        return send(src, dst, ss, rs, row=row_at(near[n - 2]), col=1)

    def own_high(n, h):
        cols = half_of(h)
        src, dst, ss, rs = pan.at[0, :, cols], win_ref.at[r - 4, :, cols], wsend.at[h, 5 + n], wrecv.at[h, r - 4]
        if n == 0:
            return send(src, dst, ss, rs, row=across, col=1)
        if n == 1:
            return send(src, dst, ss, rs, col=1)
        return send(src, dst, ss, rs, row=row_at(near[n - 2]), col=1)

    def own_low(n, h):
        cols = half_of(h)
        src, dst, ss, rs = pan.at[0, :, cols], win_ref.at[r, :, cols], wsend.at[h, 5 + n], wrecv.at[h, r]
        if n == 0:
            return send(src, dst, ss, rs, row=across)
        return send(src, dst, ss, rs, row=row_at(near[n - 1]))

    keep_low = pltpu.make_async_copy(pan.at[0], win_ref.at[y], local.at[4])
    hand = send(pan, pan, hsend, hrecv, col=1)

    def landed(i, h):
        cols = half_of(h)
        return send(pan.at[0, :, cols], win_ref.at[i, :, cols], gsend.at[h, 0], wrecv.at[h, i], col=1 - c)

    def landed_all(i):
        for h in range(2):
            landed(i, h).wait_recv()

    def pass_second(n, h):
        here = win_ref.at[4 + across, :, half_of(h)]
        return send(here, here, gsend.at[h, n], wrecv.at[h, 4 + across], row=row_at(near[n]))

    def pass_first(n, h):
        here = win_ref.at[y, :, half_of(h)]
        return send(here, here, gsend.at[h, 3 + n], wrecv.at[h, y], row=row_at(near[n]))

    def assemble(lb, h):
        valid = (lb * R + r) * B < size_ref[0]
        cols = slice(h * PW, (h + 1) * PW)

        def eight(i, carry):
            at = pl.ds(pl.multiple_of(i * 8, 8), 8)
            total = jnp.where(valid, pan[lb - 1, at, cols], 0.0)
            for s in range(F):
                mask = jnp.concatenate([got_ref[s]] * (PW // B), 1) == lb
                total = total + jnp.where(mask, inc_p[s, at, cols], 0.0)
            pan[lb - 1, at, cols] = total
            return carry

        lax.fori_loop(0, B // 8, eight, 0)

    def after(k):
        @pl.when((k == 0) & (c == 0))
        def _():
            hand_on(True)

        @pl.when((k == 1) & (c == 1))
        def _():
            for i in range(2, R):
                pivot_hand(i, False, True).wait_recv()

        for h in range(2):
            @pl.when((k == KA[h]) & (c == 0))
            def _():
                if h == 0:
                    load_panel.wait()
                for d in range(1, F):
                    contrib_panel(d, h).wait()
                assemble(2, h)
                for n in range(5):
                    own_second(n, h).start()
                assemble(1, h)

                @pl.when(r >= 4)
                def _():
                    for n in range(5):
                        own_high(n, h).start()

                @pl.when(r < 4)
                def _():
                    for n in range(4):
                        own_low(n, h).start()
                    if h == 1:
                        keep_low.start()

                if h == 1:
                    for d in range(1, F):
                        contrib_low(d).start()
                    inc_own_low.start()

                def others(lb, carry):
                    assemble(lb, h)
                    return carry

                lax.fori_loop(3, LB, others, 0)
                if h == 1:
                    hand.start()

        @pl.when((k == KC) & (c == 1))
        def _():
            for d in range(1, F):
                contrib_high(d).start()
            inc_own_high.start()

        for h in range(2):
            @pl.when((k == KF[h]) & (c == 0) & (r >= 4))
            def _():
                landed(y, h).wait_recv()
                for n in range(3):
                    pass_first(n, h).start()

            @pl.when((k == KF[h]) & (c == 1))
            def _():
                landed(4 + across, h).wait_recv()
                for n in range(3):
                    pass_second(n, h).start()

                @pl.when(r < 4)
                def _():
                    landed(y, h).wait_recv()
                    for n in range(3):
                        pass_first(n, h).start()

    cholesky_body(piv, l_ref, i_ref, x_ref, lh, ll, after)

    def solve(source, hi_ref, lo_ref, at, blocks):
        rows = slice(at * B, (at + blocks) * B)
        for k in range(PC // KD):
            o = k * KD
            cols = slice(o, o + KD)
            a = source[at : at + blocks, :, cols].reshape(blocks * B, KD)
            if k > 0:
                mine_h, mine_l = lh[cols, :o], ll[cols, :o]
                hi, lo = hi_ref[rows, :o], lo_ref[rows, :o]
                a = a - (dot_nt(hi, mine_h) + dot_nt(lo, mine_h) + dot_nt(hi, mine_l))
            hi_ref[rows, cols], lo_ref[rows, cols] = split(dot3(a, i_ref[k]))

    def out_copy(n, low):
        at = pl.ds(0, 4 * B) if low else pl.ds(0, 12 * B)
        pairs = ((ph, ph_ref), (plo, plo_ref), (wh.at[at], wh_ref.at[at]), (wl.at[at], wl_ref.at[at]))
        return pltpu.make_async_copy(*pairs[n], outs.at[n])

    @pl.when(c == 1)
    def _():
        hand.wait_recv()

    solve(pan, ph, plo, 0, 6)
    solve(pan, ph, plo, 6, 5)
    out_copy(0, False).start()
    out_copy(1, False).start()

    @pl.when(c == 0)
    def _():
        @pl.when(r < 4)
        def _():
            keep_low.wait()

        for i in range(4):
            @pl.when(y != i)
            def _():
                landed_all(i)

        solve(win_ref, wh, wl, 0, 4)
        out_copy(2, True).start()
        out_copy(3, True).start()

    @pl.when(c == 1)
    def _():
        for i in range(4):
            @pl.when((y != i) | (r >= 4))
            def _():
                landed_all(i)
        solve(win_ref, wh, wl, 0, 4)
        for half in range(2):
            for q in range(4 * half, 4 * half + 4):
                @pl.when(across != q)
                def _():
                    landed_all(4 + q)
            solve(win_ref, wh, wl, 4 * (half + 1), 4)
        out_copy(2, False).start()
        out_copy(3, False).start()

    @pl.when(c == 0)
    def _():
        for i in range(R):
            @pl.when(r == i)
            def _():
                for n in range(4):
                    pivot_copy(i, n, False).wait_send()
                    if i >= 2:
                        pivot_copy(i, n, True).wait_send()

            @pl.when(across == i)
            def _():
                for n in range(3):
                    pivot_pass(i, n, False).wait_send()
                    if i >= 2:
                        pivot_pass(i, n, True).wait_send()

            pivot_hand(i, False, False).wait_send()
            if i >= 2:
                pivot_hand(i, False, True).wait_send()
        for n in range(5):
            for h in range(2):
                own_second(n, h).wait_send()

        @pl.when(r >= 4)
        def _():
            for n in range(5):
                for h in range(2):
                    own_high(n, h).wait_send()
            for n in range(3):
                for h in range(2):
                    pass_first(n, h).wait_send()

        @pl.when(r < 4)
        def _():
            for n in range(4):
                for h in range(2):
                    own_low(n, h).wait_send()

        hand.wait_send()
        for d in range(1, F):
            contrib_low(d).wait()
        inc_own_low.wait()
        out_copy(2, True).wait()
        out_copy(3, True).wait()

    @pl.when(c == 1)
    def _():
        for n in range(3):
            for h in range(2):
                pass_second(n, h).wait_send()

        @pl.when(r < 4)
        def _():
            for n in range(3):
                for h in range(2):
                    pass_first(n, h).wait_send()

        for d in range(1, F):
            contrib_high(d).wait()
        inc_own_high.wait()
        out_copy(2, False).wait()
        out_copy(3, False).wait()

    out_copy(0, False).wait()
    out_copy(1, False).wait()


def exchange(front, contrib, dest, place, size):
    sm = pl.BlockSpec(memory_space=pltpu.SMEM)
    eight = pltpu.SemaphoreType.DMA((8,))
    one = pltpu.SemaphoreType.DMA
    own = ((LB - 1) * B, PC)
    window = (12 * B, PC)
    return pl.pallas_call(
        exchange_kernel,
        out_shape=(
            jax.ShapeDtypeStruct(own, BF16),
            jax.ShapeDtypeStruct(own, BF16),
            jax.ShapeDtypeStruct(window, BF16),
            jax.ShapeDtypeStruct(window, BF16),
            jax.ShapeDtypeStruct((F, B, HW), F32),
            jax.ShapeDtypeStruct((F, 8, B), jnp.int32),
            jax.ShapeDtypeStruct((PC, PC), F32),
        ),
        in_specs=[ANY, ANY, sm, sm, sm],
        out_specs=(ANY, ANY, ANY, ANY, ANY, VM, VM),
        scratch_shapes=[
            pltpu.VMEM((PC // KD, KD, KD), F32),
            pltpu.VMEM((NB, B, B), F32),
            pltpu.VMEM((PC, PC), BF16),
            pltpu.VMEM((PC, PC), BF16),
            pltpu.VMEM((4, B, HW), F32),
            pltpu.VMEM((F, B, HW), F32),
            pltpu.VMEM((LB - 1, B, PC), F32),
            pltpu.VMEM((12, B, PC), F32),
            pltpu.VMEM((F, B, PC), F32),
            pltpu.VMEM((R, B, PC), F32),
            pltpu.VMEM((F, 8, B), jnp.int32),
            pltpu.VMEM(own, BF16),
            pltpu.VMEM(own, BF16),
            pltpu.VMEM(window, BF16),
            pltpu.VMEM(window, BF16),
            eight,
            eight,
            eight,
            eight,
            eight,
            eight,
            pltpu.SemaphoreType.DMA((2, 8)),
            pltpu.SemaphoreType.DMA((2, 8)),
            eight,
            eight,
            eight,
            eight,
            one,
            one,
            pltpu.SemaphoreType.DMA((2, 10)),
            pltpu.SemaphoreType.DMA((2, 12)),
            pltpu.SemaphoreType.DMA((2, 6)),
            pltpu.SemaphoreType.DMA((6,)),
            pltpu.SemaphoreType.DMA((4,)),
        ],
        compiler_params=pltpu.CompilerParams(collective_id=0, has_side_effects=True, vmem_limit_bytes=62 * MIB),
    )(front, contrib, dest, place, size)


def final_kernel(meta_ref, front_ref, inc_ref, l_ref, ph, plo, wh, wl, out_ref):
    t = pl.program_id(0)
    col = meta_ref[1]
    steps = PC // KD

    @pl.when((col == 0) & (t < steps))
    def _():
        for k in range(steps):
            @pl.when(t == k)
            def _():
                cols = slice(k * KD, (k + 1) * KD)
                out_ref[0] = l_ref[:, cols]
                out_ref[1:] = (ph[:, cols].astype(F32) + plo[:, cols].astype(F32)).reshape(LB - 1, B, KD)

    @pl.when((col == 1) | (t >= steps))
    def _():
        start = pl.multiple_of((t - jnp.where(col == 0, steps, 0)) * KD, KD)
        w_hi, w_lo = wh[pl.ds(start, KD), :], wl[pl.ds(start, KD), :]
        update = dot_nt(ph[...], w_hi) + dot_nt(plo[...], w_hi) + dot_nt(ph[...], w_lo)
        out_ref[0] = jnp.zeros((B, KD), F32)
        for lb in range(1, LB):
            valid = (lb * R + meta_ref[0]) * B < meta_ref[2]
            out_ref[lb] = jnp.where(valid, front_ref[lb], 0.0) - update[(lb - 1) * B : lb * B]
        for s in range(F):
            place = meta_ref[3 + s]

            @pl.when(place >= 0)
            def _():
                out_ref[pl.ds(place, 1)] += inc_ref[s : s + 1]


def final(meta, front, inc, low, solved):
    tiles = HW // KD
    whole = dict(pipeline_mode=pl.Buffered(1))
    return pl.pallas_call(
        final_kernel,
        grid_spec=pltpu.PrefetchScalarGridSpec(
            num_scalar_prefetch=1,
            grid=(tiles,),
            in_specs=[
                pl.BlockSpec((LB, B, KD), lambda t, meta: (0, 0, t)),
                pl.BlockSpec((F, B, KD), lambda t, meta: (0, 0, t)),
                pl.BlockSpec((B, PC), lambda t, meta: (meta[0], 0), **whole),
                pl.BlockSpec(((LB - 1) * B, PC), lambda t, meta: (0, 0), **whole),
                pl.BlockSpec(((LB - 1) * B, PC), lambda t, meta: (0, 0), **whole),
                pl.BlockSpec((12 * B, PC), lambda t, meta: (0, 0), **whole),
                pl.BlockSpec((12 * B, PC), lambda t, meta: (0, 0), **whole),
            ],
            out_specs=pl.BlockSpec((LB, B, KD), lambda t, meta: (0, 0, t)),
        ),
        out_shape=jax.ShapeDtypeStruct((LB, B, HW), F32),
        compiler_params=pltpu.CompilerParams(vmem_limit_bytes=60 * MIB),
    )(meta, front, inc, low, *solved)


def on_device(front_matrix, front_sizes, contrib, dest_front, dest_local):
    front = front_matrix[0]
    *solved, inc, got, low = exchange(front, contrib[0], dest_front[0, :, 0], dest_local[0, :, 0], front_sizes)
    row_col = jnp.stack([lax.axis_index("row"), lax.axis_index("col"), front_sizes[0]]).astype(jnp.int32)
    meta = jnp.concatenate([row_col, got[:, 0, 0]])
    out = final(meta, front, inc, low, solved)
    return out[None]


def solution(mesh):
    return jax.shard_map(
        on_device,
        mesh=mesh,
        in_specs=(
            P("front", None, "row", "col"),
            P("front"),
            P("front", None, "row", "col"),
            P("front", None, "row"),
            P("front", None, "row"),
        ),
        out_specs=P("front", None, "row", "col"),
        check_vma=False,
    )
```

time: 181 us -> 159 us (0.88)
  the two profiles are of different devices: /device:TPU:31 before, /device:TPU:1 now
where the time goes in v4:
time: 159 us
  Pallas kernels  156 us (98%)
    pallas_call x1, Pallas kernels, exchange(): pl.pallas_call(exchange_kernel, out_shape=(jax.ShapeDtypeStruct(own, BF16...  134 us
    pallas_call x1, Pallas kernels, final(): pl.pallas_call(final_kernel, grid_spec=pltpu.PrefetchScalarGridSpec(num_s...  22.8 us

profile of v4, /device:TPU:1, one launch (start us, length us, event | category | flops | bytes accessed | tf_op | source)
XLA Modules:
  0.0 158.7 jit_solution(4871731392992629918)
XLA Ops:
  0.7 133.6 %shard_map.55 = (bf16[1408,1024]{1,0:T(8,128)(2,1)}, bf16[1408,1024]{1,0:T(8,128)(2,1)}, bf16[1536,1024]{1,0:T(8,128)(2,1)}, bf16[1536,1024]{1,0:T(8,128)(2,1)},...) custom-call(f32[12,128,1536]{2,1,0:T(8,128)} %bitcast.7, f32[4,128,1536]{2,1,0:T(8,128)} %bitcast.9, ...), custom_call_target="tpu_custom_call" | custom-call | tf_op jit(solution)/shard_map/pallas_call | solution.py:622
  134.2 1.0 slice_reduce_fusion
  135.2 0.6 pad_add_fusion.meta_ref
  135.8 22.8 %shard_map.56 = f32[12,128,1536]{2,1,0:T(8,128)} custom-call(s32[11]{0:T(128)} %pad_add_fusion.meta_ref, f32[12,128,1536]{2,1,0:T(8,128)} %bitcast.8, f32[8,128,1536]{2,1,0:T(8,128)} %get-tuple-element.13.inc_ref, f32[1024,1024]{1,0:T(8,128)} %get-tuple-element.14.l_ref, bf16[1408,1024]{1,0:T(8,128)(2,1)} %get-tuple-element.15.ph, ...), custom_call_target="tpu_custom_call" | custom-call | tf_op jit(solution)/shard_map/pallas_call | solution.py:709

commit v5 on v4

--- a/solution.py
+++ b/solution.py
@@ -17,7 +17,7 @@
 PW = 512
 KD = 256
 KA = (1, 3)
-KC = 0
+KC = 3
 KF = (3, 6)
 MESH = pl.DeviceIdType.MESH
 ANY = pl.BlockSpec(memory_space=pl.ANY)
@@ -293,12 +293,9 @@
             to = lax.rem(f + d, F)
             which, _ = choice(to)
             packed[to, :, :PC] = cont[which, :, :PC]
-            contrib_panel(d, 0).start()
             return carry
 
         lax.fori_loop(1, F, one, 0)
-        for d in range(1, F):
-            contrib_panel(d, 1).start()
         which, _ = choice(f)
         inc_p[f] = cont[which, :, :PC]
 
@@ -342,6 +339,8 @@
     @pl.when(c == 0)
     def _():
         hand_on(False)
+        for d in range(1, F):
+            contrib_panel(d, 0).start()
         for i in range(R):
             @pl.when(r == i)
             def _():
@@ -418,6 +417,8 @@
         @pl.when((k == 0) & (c == 0))
         def _():
             hand_on(True)
+            for d in range(1, F):
+                contrib_panel(d, 1).start()
 
         @pl.when((k == 1) & (c == 1))
         def _():

time: 159 us -> 144 us (0.906)
  Pallas kernels: 156 us -> 141 us
    pallas_call x1, Pallas kernels: 134 us -> 118 us  [exchange(): pl.pallas_call(exchange_kernel, out_shape=(jax.ShapeDtypeStruct(own, BF16...]
where the time goes in v5:
time: 144 us; the launch traced here: 143 us
  Pallas kernels  141 us (98%)
    pallas_call x1, Pallas kernels, exchange(): pl.pallas_call(exchange_kernel, out_shape=(jax.ShapeDtypeStruct(own, BF16...  118 us
    pallas_call x1, Pallas kernels, final(): pl.pallas_call(final_kernel, grid_spec=pltpu.PrefetchScalarGridSpec(num_s...  22.9 us

profile of v5, /device:TPU:1, one launch (start us, length us, event | category | flops | bytes accessed | tf_op | source)
XLA Modules:
  0.0 143.3 jit_solution(8516022143961915046)
XLA Ops:
  0.7 118.1 %shard_map.55 = (bf16[1408,1024]{1,0:T(8,128)(2,1)}, bf16[1408,1024]{1,0:T(8,128)(2,1)}, bf16[1536,1024]{1,0:T(8,128)(2,1)}, bf16[1536,1024]{1,0:T(8,128)(2,1)},...) custom-call(f32[12,128,1536]{2,1,0:T(8,128)} %bitcast.7, f32[4,128,1536]{2,1,0:T(8,128)} %bitcast.9, ...), custom_call_target="tpu_custom_call" | custom-call | tf_op jit(solution)/shard_map/pallas_call | solution.py:623
  118.8 1.0 slice_reduce_fusion
  119.8 0.6 pad_add_fusion.meta_ref
  120.4 22.9 %shard_map.56 = f32[12,128,1536]{2,1,0:T(8,128)} custom-call(s32[11]{0:T(128)} %pad_add_fusion.meta_ref, f32[12,128,1536]{2,1,0:T(8,128)} %bitcast.8, f32[8,128,1536]{2,1,0:T(8,128)} %get-tuple-element.13.inc_ref, f32[1024,1024]{1,0:T(8,128)} %get-tuple-element.14.l_ref, bf16[1408,1024]{1,0:T(8,128)(2,1)} %get-tuple-element.15.ph, ...), custom_call_target="tpu_custom_call" | custom-call | tf_op jit(solution)/shard_map/pallas_call | solution.py:710

commit v6 on v5

--- a/solution.py
+++ b/solution.py
@@ -17,7 +17,7 @@
 PW = 512
 KD = 256
 KA = (1, 3)
-KC = 3
+KC = 5
 KF = (3, 6)
 MESH = pl.DeviceIdType.MESH
 ANY = pl.BlockSpec(memory_space=pl.ANY)

time: 144 us -> 142 us (0.986)
  no operation moved by 1% of the time
where the time goes in v6:
time: 142 us
  Pallas kernels  140 us (99%)
    pallas_call x1, Pallas kernels, exchange(): pl.pallas_call(exchange_kernel, out_shape=(jax.ShapeDtypeStruct(own, BF16...  117 us
    pallas_call x1, Pallas kernels, final(): pl.pallas_call(final_kernel, grid_spec=pltpu.PrefetchScalarGridSpec(num_s...  22.7 us

profile of v6, /device:TPU:1, one launch (start us, length us, event | category | flops | bytes accessed | tf_op | source)
XLA Modules:
  0.0 141.8 jit_solution(14444567653061695788)
XLA Ops:
  0.7 116.8 %shard_map.55 = (bf16[1408,1024]{1,0:T(8,128)(2,1)}, bf16[1408,1024]{1,0:T(8,128)(2,1)}, bf16[1536,1024]{1,0:T(8,128)(2,1)}, bf16[1536,1024]{1,0:T(8,128)(2,1)},...) custom-call(f32[12,128,1536]{2,1,0:T(8,128)} %bitcast.7, f32[4,128,1536]{2,1,0:T(8,128)} %bitcast.9, ...), custom_call_target="tpu_custom_call" | custom-call | tf_op jit(solution)/shard_map/pallas_call | solution.py:623
  117.5 1.0 slice_reduce_fusion
  118.5 0.6 pad_add_fusion.meta_ref
  119.1 22.7 %shard_map.56 = f32[12,128,1536]{2,1,0:T(8,128)} custom-call(s32[11]{0:T(128)} %pad_add_fusion.meta_ref, f32[12,128,1536]{2,1,0:T(8,128)} %bitcast.8, f32[8,128,1536]{2,1,0:T(8,128)} %get-tuple-element.13.inc_ref, f32[1024,1024]{1,0:T(8,128)} %get-tuple-element.14.l_ref, bf16[1408,1024]{1,0:T(8,128)(2,1)} %get-tuple-element.15.ph, ...), custom_call_target="tpu_custom_call" | custom-call | tf_op jit(solution)/shard_map/pallas_call | solution.py:710
